TPU v7x, 32 devices: a whole 2x2x4 slice. The times are simulated.
32 devices in a mesh: tile: 16 (over z, x, core), tm: 2 (over y).
Axes of the slice: x: 2, y: 2, z: 4, core: 2. Of those that a mesh axis runs over, the one named last changes fastest.
Arguments:
- data: bfloat16 [2048, 16, 128], P('tile', 'tm'), may hold values from -8 to 8
- send_list: int32 [16, 16, 8], P('tile'), may hold values from 0 to 127
- footprint_slot: int32 [2048, 8], P('tile'), may hold values from 0 to 127, as said below
- footprint: bfloat16 [2048, 8, 128], P('tile'), may hold values from 0 to 0.053955078
- colour: int32 [2048], P('tile'), may hold values from 0 to 3, as said below
- correlation: int32 [2048, 8], P('tile'), may hold values from 0 to 2047, as said below
- correlation_gram: float32 [2048, 8], P('tile'), may hold values from 0.01 to 0.15
- traces_init: float32 [16, 2048], P('tm', 'tile'), may hold values from 0 to 4
Outputs:
- traces: float32 [16, 2048], P('tm', 'tile')
- trace_rms: float32 [2048], P('tile')
Inputs may be any that keep to these rules, and one draw needn't show every extreme that they name: footprint_slot[k, j] names the slot c = footprint_slot[k, j] % 8 in which tile device footprint_slot[k, j] // 8 sends a block to the owner of k, tile device k // 128; the 8 slots of one footprint differ. Each tile device owns exactly a quarter of its 128 components in each colour; every listed neighbour has a colour other than the component's own. `correlation`: the tile axis folds the slab's two halves end to end, so the neighbours of a component owned by tile device d are owned by tile device d - 1, d, d + 1 or (d + 8) modulo 16; entries may repeat.
All inputs are finite; a program needn't handle non-finite values.
Results may differ from a plain program's by a relative error of at most 0.0003.
Values may be sent and summed in bfloat16 or wider, within the bound.
No kernel may reach another device: no remote copies, remote signals or barrier semaphores. Data moves between devices by JAX's collectives and lax.ppermute only.
A program may use at most 64 MiB of HBM per device.

v0:
```python
import jax
import jax.numpy as jnp
from jax import lax
from jax.sharding import PartitionSpec as P


def shards(
    data, send_list, footprint_slot, footprint, colour, correlation, correlation_gram, traces_init
):
    tile_count = lax.axis_size("tile")
    tile_here = lax.axis_index("tile")
    comp_count = colour.shape[0]
    quarter = comp_count // 4
    frames_dev = data.shape[1]
    voxels = data.shape[2]
    cap_slots = send_list.shape[2]
    slot_count = tile_count * cap_slots
    blocks_fp = footprint.shape[1]
    listed = correlation.shape[1]
    outgoing = data[send_list[0].reshape(-1)].reshape(tile_count, cap_slots, frames_dev, voxels)
    arrived = lax.all_to_all(outgoing, "tile", split_axis=0, concat_axis=0, tiled=True).reshape(
        slot_count, frames_dev, voxels
    )
    weights32 = footprint.astype(jnp.float32)
    self_gram = jnp.sum(weights32 * weights32, axis=(1, 2))
    comp_block = min(32, comp_count)
    block_total = comp_count // comp_block
    slot_range = jnp.arange(slot_count, dtype=jnp.int32)

    def project(inputs):
        slot_ids, weight_rows = inputs
        one_hot = (slot_ids[:, :, None] == slot_range[None, None, :]).astype(jnp.bfloat16)
        spread = jnp.einsum(
            "kjs,kjv->svk", one_hot, weight_rows, preferred_element_type=jnp.bfloat16
        )
        return jnp.einsum("sfv,svk->fk", arrived, spread, preferred_element_type=jnp.float32)

    pieces = lax.map(
        project,
        (
            footprint_slot.reshape(block_total, comp_block, blocks_fp),
            footprint.reshape(block_total, comp_block, blocks_fp, voxels),
        ),
    )
    projected = jnp.transpose(pieces, (1, 0, 2)).reshape(frames_dev, comp_count)
    ordering = jnp.argsort(colour, stable=True)
    grouped = jnp.argsort(ordering)
    rank_in = grouped % quarter
    proj_group = projected[:, ordering].reshape(frames_dev, 4, quarter)
    gram_group = self_gram[ordering].reshape(4, quarter)
    nb_group = correlation[ordering].reshape(4, quarter, listed)
    weight_group = correlation_gram[ordering].reshape(4, quarter, listed)
    start_group = traces_init[:, ordering].reshape(frames_dev, 4, quarter)
    own_flat = colour * (tile_count * quarter) + tile_here * quarter + rank_in
    table, flat_all = (
        lax.all_gather(start_group, "tile", axis=2, tiled=True),
        lax.all_gather(own_flat, "tile", axis=0, tiled=True),
    )
    span_width = tile_count * quarter
    lookup = flat_all[nb_group]
    fresh_parts = []
    for step_colour in range(4):
        flat_table = table.reshape(frames_dev, 4 * span_width)
        values = jnp.take(flat_table, lookup[step_colour].reshape(-1), axis=1).reshape(
            frames_dev, quarter, listed
        )
        neighbour_sum = jnp.sum(values * weight_group[step_colour][None, :, :], axis=2)
        fresh = jnp.maximum(
            (proj_group[:, step_colour, :] - neighbour_sum) / gram_group[step_colour][None, :], 0.0
        )
        fresh_parts.append(fresh)
        if step_colour + 1 < 4:
            arrived_colour = lax.all_gather(fresh, "tile", axis=1, tiled=True)
            table = table.at[:, step_colour, :].set(arrived_colour)
    final_group = jnp.stack(fresh_parts, axis=1).reshape(frames_dev, comp_count)
    traces = final_group[:, grouped]
    energy_sum = lax.psum(jnp.sum(traces * traces, axis=0), "tm")
    trace_rms = jnp.sqrt(energy_sum / (frames_dev * lax.axis_size("tm")) + 1e-06)
    return (traces, trace_rms)


def solution(mesh):
    placed = (
        P("tile", "tm", None),
        P("tile", None, None),
        P("tile", None),
        P("tile", None, None),
        P("tile"),
        P("tile", None),
        P("tile", None),
        P("tm", "tile"),
    )
    return jax.shard_map(
        shards, mesh=mesh, in_specs=placed, out_specs=(P("tm", "tile"), P("tile")), check_vma=False
    )
```

profile of v0, /device:TPU:0, one launch (start us, length us, event | category | flops | bytes accessed | tf_op | source)
XLA Modules:
  0.0 153.4 jit_solution(15843018522794582634)
XLA Ops:
  0.6 0.8 copy.83
  1.6 1.4 gather_fusion
  3.0 7.4 %all-to-all-start = ((bf16[16,8,8,128]{3,2,1,0:T(8,128)(2,1)}), bf16[16,8,8,128]{3,2,1,0:T(8,128)(2,1)S(1)}, u32[]{:S(2)}, u32[]{:S(2)}) async-start(bf16[16,8,8,128]{3,2,1,0:T(8,128)(2,1)} %bitcast.2), calls=%async_computation | async-start | bytes 524288 | tf_op jit(solution)/shard_map/all_to_all | solution.py:21
  11.0 2.5 %sort.34 = (s32[128]{0:T(128)}, s32[128]{0:T(128)S(1)}) sort(s32[128]{0:T(128)S(1)} %copy-done.7, s32[128]{0:T(128)S(1)} %iota.12), dimensions={0}, to_apply=%region_2.3 | sort | flops 896 | bytes 2048 | tf_op jit(solution)/shard_map/jit(argsort)/sort | solution.py:46
  13.6 2.5 %sort.35 = (s32[128]{0:T(128)}, s32[128]{0:T(128)S(1)}) sort(s32[128]{0:T(128)S(1)} %get-tuple-element.74, s32[128]{0:T(128)S(1)} %iota.13), dimensions={0}, to_apply=%region_3.4 | sort | flops 896 | bytes 2048 | tf_op jit(solution)/shard_map/jit(argsort)/sort | solution.py:47
  16.1 21.6 %all-gather = s32[16,1,128]{2,1,0:T(1,128)S(1)} all-gather(s32[1,1,128]{2,1,0:T(1,128)S(1)} %get-tuple-element.152), channel_id=1, replica_groups=mesh['tile'=16,'tm'=2] {'tile'}, dimensions={0}, use_global_device_ids=true | all-gather | bytes 8704 | tf_op jit(solution)/shard_map/all_gather | solution.py:57
  37.8 0.6 gather_fusion.3
  38.6 6.2 %gather_fusion.4 = s32[1024]{0:T(1024)S(1)} fusion(s32[2048]{0:T(1024)S(1)} %bitcast.155, s32[1024]{0:T(1024)S(1)} %broadcast_clamp_fusion), kind=kCustom, calls=%fused_computation.8 | custom fusion | bytes 12288 | tf_op jit(solution)/shard_map/gather | solution.py:60
  44.8 1.0 multiply_reduce_fusion
  45.9 0.7 copy-done.4
  47.3 1.2 gather_fusion.6
  49.4 0.6 gather_fusion.2
  50.0 20.5 %all_gather.15 = f32[8,4,512]{0,2,1:T(8,128)S(1)} all-gather(f32[8,4,32]{0,2,1:T(8,128)S(1)} %bitcast.171), channel_id=1, replica_groups=mesh['tile'=16,'tm'=2] {'tile'}, dimensions={2}, use_global_device_ids=true | all-gather | bytes 69632 | tf_op jit(solution)/shard_map/all_gather | solution.py:56
  70.5 0.7 gather_fusion.8
  71.5 8.1 %while.14 = (s32[]{:T(128)}, f32[4,8,32]{2,1,0:T(8,128)S(1)}, bf16[4,32,8,128]{3,2,1,0:T(8,128)(2,1)S(1)}, s32[4,32,8]{1,0,2:T(4,128)S(1)}, bf16[128,8,128]{2,1,0:T(8,128)(2,1)S(1)}, /*index=5*/s32[]{:T(128)}) while((s32[]{:T(128)}, f32[4,8,32]{2,1,0:T(8,128)S(1)}, bf16[4,32,8,128]{3,2,1,0:T(8,128)(2,1)S(1)}, ...), condition=%wide.region_1.2_spmd.clone, body=%wide.region_0.0_spmd.clone.sunk | while | flops 16809984 | bytes 4546649 | solution.py:38
  72.2 1.0 copy.103
  74.2 1.0 copy.103
  76.2 1.0 copy.103
  78.3 1.0 copy.103
  79.7 0.7 gather_fusion.1
  80.5 19.9 %all-gather.1 = f32[16,32,8]{1,2,0:T(8,128)S(1)} all-gather(f32[1,32,8]{1,2,0:T(8,128)S(1)} %copy.89), channel_id=1, replica_groups=mesh['tile'=16,'tm'=2] {'tile'}, dimensions={0}, use_global_device_ids=true | all-gather | bytes 17408 | tf_op jit(solution)/shard_map/all_gather | solution.py:73
  100.7 0.7 constant_dynamic-update-slice_fusion.2
  101.4 1.9 %gather_fusion.9 = f32[256,8]{1,0:T(8,128)S(1)} fusion(f32[8,2048]{0,1:T(8,128)} %bitcast.158, s32[1024]{0:T(1024)S(1)} %pad_clamp_fusion.3), kind=kCustom, calls=%fused_computation.1.clone | custom fusion | bytes 17408 | tf_op jit(solution)/shard_map/jit(_take)/gather | solution.py:64
  103.6 17.6 %all-gather.2 = f32[16,32,8]{1,2,0:T(8,128)S(1)} all-gather(f32[1,32,8]{1,2,0:T(8,128)S(1)} %copy.92), channel_id=1, replica_groups=mesh['tile'=16,'tm'=2] {'tile'}, dimensions={0}, use_global_device_ids=true | all-gather | bytes 17408 | tf_op jit(solution)/shard_map/all_gather | solution.py:73
  121.5 0.7 constant_dynamic-update-slice_fusion.1
  122.2 1.9 %gather_fusion.10 = f32[256,8]{1,0:T(8,128)S(1)} fusion(f32[8,2048]{0,1:T(8,128)} %bitcast.159, s32[1024]{0:T(1024)S(1)} %pad_clamp_fusion.2), kind=kCustom, calls=%fused_computation.2.clone | custom fusion | bytes 17408 | tf_op jit(solution)/shard_map/jit(_take)/gather | solution.py:64
  124.4 18.9 %all-gather.3 = f32[16,32,8]{1,2,0:T(8,128)S(1)} all-gather(f32[1,32,8]{1,2,0:T(8,128)S(1)} %copy.95), channel_id=1, replica_groups=mesh['tile'=16,'tm'=2] {'tile'}, dimensions={0}, use_global_device_ids=true | all-gather | bytes 17408 | tf_op jit(solution)/shard_map/all_gather | solution.py:73
  143.6 0.7 constant_dynamic-update-slice_fusion
  144.3 1.9 %gather_fusion.11 = f32[256,8]{1,0:T(8,128)S(1)} fusion(f32[8,2048]{0,1:T(8,128)} %bitcast.160, s32[1024]{0:T(1024)S(1)} %pad_clamp_fusion.1), kind=kCustom, calls=%fused_computation.3.clone | custom fusion | bytes 17408 | tf_op jit(solution)/shard_map/jit(_take)/gather | solution.py:64
  146.5 0.6 gather_fusion.7
  147.3 4.9 %psum.7 = f32[128]{0:T(128)S(1)} all-reduce(f32[128]{0:T(128)S(1)} %multiply_reduce_fusion.1), channel_id=1, replica_groups=mesh['tile'=16,'tm'=2] {'tm'}, use_global_device_ids=true, to_apply=%region_10.12 | all-reduce | flops 128 | bytes 1024 | tf_op jit(solution)/shard_map/psum | solution.py:77
  152.8 0.7 copy.98
  (81 shorter events, 9.3 us)
Async XLA Ops:
  0.6 1.0 copy-start
  3.0 68.5 %all-to-all-start = ((bf16[16,8,8,128]{3,2,1,0:T(8,128)(2,1)}), bf16[16,8,8,128]{3,2,1,0:T(8,128)(2,1)S(1)}, u32[]{:S(2)}, u32[]{:S(2)}) async-start(bf16[16,8,8,128]{3,2,1,0:T(8,128)(2,1)} %bitcast.2), calls=%async_computation | async-start | bytes 524288 | tf_op jit(solution)/shard_map/all_to_all | solution.py:21
  10.4 0.7 copy-start.7
  16.1 21.6 %copy-start.3 = (s32[128,8]{0,1:T(8,128)S(1)}, s32[128,8]{0,1:T(8,128)}, u32[]{:S(2)}) copy-start(s32[128,8]{0,1:T(8,128)} %param.23) | copy-start | bytes 12292
  38.6 6.2 %copy-start.2 = (bf16[128,8,128]{2,1,0:T(8,128)(2,1)S(1)}, bf16[128,8,128]{2,1,0:T(8,128)(2,1)}, u32[]{:S(2)}) copy-start(bf16[128,8,128]{2,1,0:T(8,128)(2,1)} %param.21) | copy-start | bytes 786436
  45.9 0.7 copy-start.4
  47.3 1.2 copy-start.5
  48.6 0.7 copy-start.6
  70.5 1.0 copy-start.1
where the time goes:
time: 154 us; the launch traced here: 153 us
  blocking collectives  103 us (67%)
  local copies, waits for them, and re-layouts  30.1 us (20%)
  other arithmetic  7.73 us (5%)
  starting transfers between devices  7.36 us (5%)
  matrix products  3.74 us (2%)
    all_gather x3, blocking collectives, shards(): arrived_colour = lax.all_gather(fresh, 'tile', axis=1, tiled=True)  56.5 us
    all_gather x1, blocking collectives, shards(): lax.all_gather(own_flat, 'tile', axis=0, tiled=True)  21.6 us
    all_gather x1, blocking collectives, shards(): lax.all_gather(start_group, 'tile', axis=2, tiled=True)  20.5 us
    all_to_all x1, starting transfers between devices, shards(): lax.all_to_all(outgoing, 'tile', split_axis=0, concat_axis=0, tiled=True)  7.36 us
    gather x4, local copies, waits for them, and re-layouts, shards(): jnp.take(flat_table, lookup[step_colour].reshape(-1), axis=1)  6.56 us
    gather x1, local copies, waits for them, and re-layouts, shards(): lookup = flat_all[nb_group]  6.15 us
    psum x1, blocking collectives, shards(): energy_sum = lax.psum(jnp.sum(traces * traces, axis=0), 'tm')  4.94 us
    unnamed x27, local copies, waits for them, and re-layouts  4.23 us
  transfers between devices with their start and end apart: 1, of which 0 were waited for; matrix products, arithmetic and copies ran while one was open for 11% of the time, Pallas kernels for 0%

commit v1 on v0

v1 whole, which is shorter than its diff:
```python
import functools

import jax
import jax.numpy as jnp
from jax import lax
from jax.experimental import pallas as pl
from jax.experimental.pallas import tpu as pltpu
from jax.sharding import PartitionSpec as P

REACH = (
    (0, 0), (1, 0), (-1, 0), (0, 1),
    (1, 1), (-1, 1), (2, 0), (-2, 0),
    (3, 0), (-3, 0), (2, 1), (-2, 1),
)
NEAR = REACH[:4]
LANES = 128
QUARTER = 32
DATA_ROWS = 64
META_ROWS = 32
VMEM_LIMIT = 48 * 2 ** 20
NT = (((1,), (1,)), ((), ()))


def iota(shape, dim):
    return lax.broadcasted_iota(jnp.int32, shape, dim)


def reach_at(device, near):
    return REACH.index((device[0] + near[0], (device[1] + near[1]) % 2))


def tile_at(me, rel, n):
    return lax.rem(me + rel[0] + rel[1] * (n // 2) + n, n)


def dot(a, b):
    return jnp.dot(a, b, preferred_element_type=jnp.float32)


def dot_nt(a, b):
    return lax.dot_general(a, b, NT, preferred_element_type=jnp.float32)


def split2(x):
    hi = x.astype(jnp.bfloat16).astype(jnp.float32)
    return hi, x - hi


def split3(x):
    hi, rest = split2(x)
    mid, low = split2(rest)
    return jnp.concatenate([hi, mid, low], axis=0).astype(jnp.bfloat16)


def join3(y):
    rows = y.shape[0] // 3
    return y[:rows] + y[rows : 2 * rows] + y[2 * rows :]


def dot_split(x, b_hi, b_lo):
    hi, low = split2(x)
    rows = x.shape[0]
    both = dot(jnp.concatenate([hi, low], axis=0).astype(jnp.bfloat16), b_hi)
    return both[:rows] + both[rows:] + dot(hi.astype(jnp.bfloat16), b_lo)


def put_split(hi_ref, lo_ref, x, place=slice(None)):
    hi, low = split2(x)
    hi_ref[place, :] = hi.astype(jnp.bfloat16)
    lo_ref[place, :] = low.astype(jnp.bfloat16)


def places(colour_row):
    in_class = colour_row == iota((8, LANES), 0)
    before = (iota((LANES, LANES), 0) < iota((LANES, LANES), 1)).astype(jnp.bfloat16)
    counts = dot(in_class.astype(jnp.bfloat16), before)
    rank = jnp.sum(jnp.where(in_class, counts, 0.0), axis=0, keepdims=True)
    return rank + (colour_row * QUARTER).astype(jnp.float32)


def pack_kernel(n, send_ref, data_ref, colour_ref, corr_ref, gram_ref, init_ref, out_ref, own_ref):
    me = lax.axis_index("tile")
    lane = iota((8, LANES), 1)
    row = iota((8, LANES), 0)
    pos = places(colour_ref[...])
    order = (iota((LANES, LANES), 0).astype(jnp.float32) == pos).astype(jnp.bfloat16)
    ids = corr_ref[...]
    away = jnp.bitwise_and(lax.shift_right_logical(ids, 7) - me, n - 1)
    which = jnp.where(away == 0, 0, jnp.where(away == 1, 1, jnp.where(away == n - 1, 2, 3)))
    code = which * LANES + jnp.bitwise_and(ids, LANES - 1) - 2 * LANES
    gram_hi, gram_lo = split2(gram_ref[...])
    init_hi, init_lo = split2(init_ref[...])
    rows = [code.astype(jnp.float32), gram_hi, gram_lo, init_hi, init_lo, lane.astype(jnp.float32)]
    placed = dot_nt(jnp.concatenate(rows, axis=0).astype(jnp.bfloat16), order)
    code, gram_hi, gram_lo, init_hi, init_lo, ident = [placed[8 * i : 8 * i + 8] for i in range(6)]
    own_ref[0:8, :] = code
    own_ref[8:16, :] = gram_hi + gram_lo
    own_ref[16:24, :] = jnp.broadcast_to(pos, (8, LANES))
    first = jnp.where(lane < 64, pltpu.roll(code, 96, 1), pltpu.roll(gram_hi, 32, 1))
    named = jnp.where(row == 0, pltpu.roll(ident, 64, 1), ident)
    second = jnp.where(lane < 64, pltpu.roll(gram_lo, 96, 1), named)
    meta = jnp.concatenate([first, second, init_hi, init_lo], axis=0).astype(jnp.bfloat16)
    for target in range(n):
        out_ref[target, DATA_ROWS:, :] = meta
        blocks = [data_ref[send_ref[c, target]].astype(jnp.float32) for c in range(8)]
        out_ref[target, :DATA_ROWS, :] = jnp.concatenate(blocks, axis=0).astype(jnp.bfloat16)


def names_column(meta):
    lane = iota((1, LANES), 1)
    named = jnp.where(lane < 64, pltpu.roll(meta[8:9], 64, 1), meta[9:10])
    eye = iota((LANES, LANES), 0) == iota((LANES, LANES), 1)
    spread = jnp.where(eye, named, 0.0).astype(jnp.bfloat16)
    return dot(spread, jnp.ones((LANES, LANES), jnp.bfloat16))


def listed(names, codes, weights):
    total = None
    for i in range(codes.shape[0]):
        term = jnp.where(names == codes[i : i + 1], weights[i : i + 1], 0.0)
        total = term if total is None else total + term
    return total


def project_kernel(n, tm, recv_ref, fp_ref, slot_ref, own_ref, out_ref, sg_ref, a3h_ref, a3l_ref):
    me = lax.axis_index("tile")
    lane = iota((8, LANES), 1)
    row = iota((8, LANES), 0)
    wide = 8 * LANES
    widen = (lax.shift_right_logical(iota((LANES, wide), 1), 3) == iota((LANES, wide), 0)).astype(jnp.bfloat16)
    narrow = jnp.concatenate([slot_ref[...].astype(jnp.float32), own_ref[16:24, :]], axis=0)
    if n * 8 <= 256:
        wider = dot(narrow.astype(jnp.bfloat16), widen)
    else:
        wider = join3(dot(split3(narrow), widen))
    mine = jnp.bitwise_and(iota((8, wide), 1), 7) == iota((8, wide), 0)
    slot_row = jnp.sum(jnp.where(mine, wider[0:8], 0.0), axis=0, keepdims=True)
    slot_row = jnp.broadcast_to(slot_row, (8, wide))
    order = (iota((LANES, wide), 0).astype(jnp.float32) == wider[8:9]).astype(jnp.bfloat16)
    weights = fp_ref[...]
    total = jnp.zeros((8, wide), jnp.float32)
    group = 4
    for source in range(0, n, group):
        blocks = recv_ref[source : source + group, :DATA_ROWS, :].reshape(group * DATA_ROWS, LANES)
        product = dot_nt(blocks, weights)
        for c in range(group * 8):
            hit = slot_row == float(source * 8 + c)
            total = total + jnp.where(hit, product[8 * c : 8 * c + 8], 0.0)
    wide32 = weights.astype(jnp.float32)
    square_hi, square_lo = split2(wide32 * wide32)
    ones = jnp.ones((8, LANES), jnp.bfloat16)
    squares = dot_nt(ones, square_hi.astype(jnp.bfloat16)) + dot_nt(ones, square_lo.astype(jnp.bfloat16))
    placed = join3(dot_nt(split3(jnp.concatenate([total, squares], axis=0)), order))
    projected, gram = placed[0:8], placed[8:16]
    sg_ref[...] = gram
    codes, grams = own_ref[0:8, :], own_ref[8:16, :]
    after = lax.shift_right_logical(iota((LANES, LANES), 0), 5) > lax.shift_right_logical(iota((LANES, LANES), 1), 5)
    coefs, starts = [], []
    for r, rel in enumerate(NEAR):
        meta = recv_ref[tile_at(me, rel, n), DATA_ROWS:, :].astype(jnp.float32)
        names = names_column(meta) + float(r * LANES - 2 * LANES)
        coefs.append(listed(names, codes, grams))
        starts.append(meta[16:24] + meta[24:32])
    late = jnp.concatenate([jnp.where(after, coef, 0.0) for coef in coefs], axis=0)
    late_hi, late_lo = split2(late)
    held = dot_split(
        jnp.concatenate(starts, axis=1), late_hi.astype(jnp.bfloat16), late_lo.astype(jnp.bfloat16)
    )
    for c in range(3):
        for p in range(4):
            source = coefs[(p - c) % 4][c * QUARTER : (c + 1) * QUARTER]
            start = c * LANES + p * QUARTER
            put_split(a3h_ref, a3l_ref, source, slice(start, start + QUARTER))
    base = projected - held
    message = jnp.where(lane < QUARTER, jnp.maximum(base / gram, 0.0), base)
    grams12 = jnp.where(row == 0, pltpu.roll(gram, 64, 1), pltpu.roll(gram, 32, 1))
    others = jnp.where(lane < 96, message, grams12)
    for t in range(n * tm):
        out_ref[t] = others
    for i, rel in enumerate(REACH):
        source = message if i == 0 else others
        turned = source if i % 4 == 0 else pltpu.roll(source, QUARTER * (i % 4), 1)
        target = tile_at(me, (-rel[0], rel[1]), n)
        for t in range(tm):
            out_ref[target * tm + t] = turned


def coef_kernel(n, recv_ref, a1h_ref, a1l_ref, a2h_ref, a2l_ref):
    me = lax.axis_index("tile")
    block = lax.shift_right_logical(iota((8, LANES), 1), 5)
    names, codes, gram_hi, gram_lo = [], [], [], []
    for i, rel in enumerate(REACH):
        meta = recv_ref[tile_at(me, rel, n), DATA_ROWS:, :].astype(jnp.float32)
        names.append(names_column(meta) + float(i * LANES))
        if i < 8:
            code = meta[0:8].astype(jnp.int32) + 2 * LANES
            which = lax.shift_right_logical(code, 7)
            at = [reach_at(rel, near) for near in NEAR]
            place = jnp.where(
                which == 0, at[0], jnp.where(which == 1, at[1], jnp.where(which == 2, at[2], at[3]))
            )
            code = place * LANES + jnp.bitwise_and(code, LANES - 1)
            codes.append(code.astype(jnp.float32))
            gram_hi.append(meta[0:8])
            gram_lo.append(meta[8:16])

    def gathered(parts, group, colour, start):
        out = None
        for q in range(4):
            p = (q + colour) % 4
            shift = (QUARTER * p - start) % LANES
            turned = parts[4 * group + q]
            turned = turned if shift == 0 else pltpu.roll(turned, shift, 1)
            out = turned if out is None else jnp.where(block == p, turned, out)
        return out

    first = jnp.concatenate([name[0:QUARTER] for name in names], axis=0)
    for group in range(2):
        code = gathered(codes, group, 1, 0)
        gram = gathered(gram_hi, group, 1, 64) + gathered(gram_lo, group, 1, 0)
        hi, low = split2(listed(first, code, gram))
        a1h_ref[:, group * LANES : (group + 1) * LANES] = hi.astype(jnp.bfloat16)
        a1l_ref[:, group * LANES : (group + 1) * LANES] = low.astype(jnp.bfloat16)
    earlier = [name[0:QUARTER] for name in names[:8]]
    for group in range(2):
        earlier += [names[4 * group + (p - 1) % 4][QUARTER : 2 * QUARTER] for p in range(4)]
    code = gathered(codes, 0, 2, 32)
    gram = gathered(gram_hi, 0, 2, 96) + gathered(gram_lo, 0, 2, 32)
    put_split(a2h_ref, a2l_ref, listed(jnp.concatenate(earlier, axis=0), code, gram))


def sweep_kernel(
    n, tm, recv_ref, sg_ref, own_ref, a1h_ref, a1l_ref, a2h_ref, a2l_ref, a3h_ref, a3l_ref, traces_ref, rms_ref
):
    me = lax.axis_index("tile")
    frames = 8 * tm
    block = lax.shift_right_logical(iota((frames, LANES), 1), 5)
    messages = []
    for rel in REACH:
        first = tile_at(me, rel, n) * tm
        messages.append(jnp.concatenate([recv_ref[first + t] for t in range(tm)], axis=0))

    def gathered(group, turn):
        out = messages[4 * group]
        for q in range(4):
            if q or turn:
                out = jnp.where(block == (q + turn) % 4, messages[4 * group + q], out)
        return out

    gram = sg_ref[0:1, :]
    first_lane = iota((1, LANES), 1)

    def gram_of(group, colour):
        rows = gathered(group, 3)[colour - 1 : colour]
        rows = pltpu.roll(rows, 64 if colour == 1 else 96, 1)
        if group:
            return rows
        own = lax.shift_right_logical(first_lane, 5) == colour
        return jnp.where(own, gram, rows)

    x0 = [gathered(group, 0) for group in range(3)]
    n1 = dot_split(jnp.concatenate(x0, axis=1), a1h_ref[...], a1l_ref[...])
    x1 = [
        jnp.maximum((gathered(g, 1) - n1[:, g * LANES : (g + 1) * LANES]) / gram_of(g, 1), 0.0) for g in range(2)
    ]
    n2 = dot_split(jnp.concatenate([x0[0], x0[1], x1[0], x1[1]], axis=1), a2h_ref[...], a2l_ref[...])
    x2 = jnp.maximum((gathered(0, 2) - n2) / gram_of(0, 2), 0.0)
    n3 = dot_split(jnp.concatenate([x0[0], x1[0], x2], axis=1), a3h_ref[...], a3l_ref[...])
    x3 = jnp.maximum((messages[0] - n3) / gram, 0.0)
    own = jnp.where(
        block == 0, messages[0], jnp.where(block == 1, x1[0], jnp.where(block == 2, x2, x3))
    )
    energy = jnp.sum(own * own, axis=0, keepdims=True)
    half = lax.axis_index("tm")
    mine = own[0:8]
    for t in range(1, tm):
        mine = jnp.where(half == t, own[8 * t : 8 * t + 8], mine)
    order = (iota((LANES, LANES), 0).astype(jnp.float32) == own_ref[16:17, :]).astype(jnp.bfloat16)
    stacked = jnp.concatenate([mine, jnp.broadcast_to(energy, (8, LANES))], axis=0)
    placed = join3(dot(split3(stacked), order))
    traces_ref[...] = placed[0:8]
    rms_ref[...] = jnp.sqrt(placed[8:9] / frames + 1e-06)


def shards(
    data, send_list, footprint_slot, footprint, colour, correlation, correlation_gram, traces_init
):
    n = lax.axis_size("tile")
    tm = lax.axis_size("tm")
    f32, bf16 = jnp.float32, jnp.bfloat16
    shape = jax.ShapeDtypeStruct
    params = pltpu.CompilerParams(vmem_limit_bytes=VMEM_LIMIT)
    vmem = pl.BlockSpec(memory_space=pltpu.VMEM)
    smem = pl.BlockSpec(memory_space=pltpu.SMEM)

    def call(body, outs, ins):
        return pl.pallas_call(
            body, out_shape=outs, in_specs=ins, out_specs=[vmem] * len(outs), compiler_params=params
        )

    outgoing, own = call(
        functools.partial(pack_kernel, n),
        [shape((n, DATA_ROWS + META_ROWS, LANES), bf16), shape((24, LANES), f32)],
        [smem] + [vmem] * 5,
    )(send_list[0].T, data, colour.reshape(1, LANES), correlation.T, correlation_gram.T, traces_init)
    arrived = lax.all_to_all(outgoing, "tile", split_axis=0, concat_axis=0, tiled=True)
    message, self_gram, a3h, a3l = call(
        functools.partial(project_kernel, n, tm),
        [shape((n * tm, 8, LANES), f32), shape((8, LANES), f32)] + [shape((384, LANES), bf16)] * 2,
        [vmem] * 4,
    )(arrived, footprint.reshape(8 * LANES, LANES), footprint_slot.T, own)
    messages = lax.all_to_all(message, ("tile", "tm"), split_axis=0, concat_axis=0, tiled=True)
    a1h, a1l, a2h, a2l = call(
        functools.partial(coef_kernel, n),
        [shape((384, 2 * LANES), bf16)] * 2 + [shape((512, LANES), bf16)] * 2,
        [vmem],
    )(arrived)
    traces, rms = call(
        functools.partial(sweep_kernel, n, tm),
        [shape((8, LANES), f32), shape((1, LANES), f32)],
        [vmem] * 9,
    )(messages, self_gram, own, a1h, a1l, a2h, a2l, a3h, a3l)
    return (traces, rms.reshape(LANES))


def solution(mesh):
    placed = (
        P("tile", "tm", None),
        P("tile", None, None),
        P("tile", None),
        P("tile", None, None),
        P("tile"),
        P("tile", None),
        P("tile", None),
        P("tm", "tile"),
    )
    return jax.shard_map(
        shards, mesh=mesh, in_specs=placed, out_specs=(P("tm", "tile"), P("tile")), check_vma=False
    )
```

time: 154 us -> 41.3 us (0.27)
  blocking collectives: 103 us -> 19.5 us
  local copies, waits for them, and re-layouts: 30.1 us -> 4.37 us
  other arithmetic: 7.73 us -> 0 us
  waiting for transfers between devices: 0.01 us -> 7.73 us
  Pallas kernels: 0 us -> 5.18 us
  starting transfers between devices: 7.36 us -> 3.46 us
  matrix products: 3.74 us -> 0 us
    all_gather x5 -> x0, blocking collectives: 98.6 us -> none  [the longest x3 56.5 us: shards(): arrived_colour = lax.all_gather(fresh, 'tile', axis=1, tiled=True)]
    all_to_all x0 -> x1, blocking collectives: none -> 19.5 us  [shards(): lax.all_to_all(outgoing, 'tile', split_axis=0, concat_axis=0, tiled=True)]
    gather x12 -> x0, local copies, waits for them, and re-layouts: 18.6 us -> none  [the longest x4 6.56 us: shards(): jnp.take(flat_table, lookup[step_colour].reshape(-1), axis=1)]
    all_to_all x1, waiting for transfers between devices: 0.01 us -> 7.73 us  [shards(): lax.all_to_all(message, ('tile', 'tm'), split_axis=0, concat_axis=0, tile...]
    pallas_call x0 -> x4, Pallas kernels: none -> 5.18 us  [the longest x1 2.06 us: shards(): call(functools.partial(project_kernel, n, tm), [shape((n * tm, 8, LANES),...]
    sort x2 -> x0, other arithmetic: 5.07 us -> none  [the longest x1 2.54 us: shards(): grouped = jnp.argsort(ordering)]
    psum x1 -> x0, blocking collectives: 4.94 us -> none  [shards(): energy_sum = lax.psum(jnp.sum(traces * traces, axis=0), 'tm')]
    transpose x5 -> x0, local copies, waits for them, and re-layouts: 3.98 us -> none  [the longest x4 3.9 us: project(): jnp.einsum('kjs,kjv->svk', one_hot, weight_rows, preferred_element_type=j...]
  transfers between devices with their start and end apart: 1 -> 1, of which waited for: 0 -> 1; matrix products, arithmetic and copies ran while one was open for 11% -> 0% of each run, Pallas kernels for 0% -> 2%
where the time goes in v1:
time: 41.3 us; the launch traced here: 40.9 us
  blocking collectives  19.5 us (47%)
  waiting for transfers between devices  7.73 us (19%)
  Pallas kernels  5.18 us (13%)
  local copies, waits for them, and re-layouts  4.37 us (11%)
  starting transfers between devices  3.46 us (8%)
  between operations  0.69 us (2%)
    all_to_all x1, blocking collectives, shards(): lax.all_to_all(outgoing, 'tile', split_axis=0, concat_axis=0, tiled=True)  19.5 us
    all_to_all x1, waiting for transfers between devices, shards(): lax.all_to_all(message, ('tile', 'tm'), split_axis=0, concat_axis=0, tile...  7.73 us
    unnamed x16, local copies, waits for them, and re-layouts  4.37 us
    all_to_all x1, starting transfers between devices, shards(): lax.all_to_all(message, ('tile', 'tm'), split_axis=0, concat_axis=0, tile...  3.46 us
    pallas_call x1, Pallas kernels, shards(): call(functools.partial(project_kernel, n, tm), [shape((n * tm, 8, LANES),...  2.06 us
    pallas_call x1, Pallas kernels, shards(): call(functools.partial(sweep_kernel, n, tm), [shape((8, LANES), f32), sha...  1.24 us
    pallas_call x1, Pallas kernels, shards(): call(functools.partial(pack_kernel, n), [shape((n, DATA_ROWS + META_ROWS,...  0.99 us
    pallas_call x1, Pallas kernels, shards(): call(functools.partial(coef_kernel, n), [shape((384, 2 * LANES), bf16)] *...  0.89 us
  transfers between devices with their start and end apart: 1, of which 1 were waited for; matrix products, arithmetic and copies ran while one was open for 0% of the time, Pallas kernels for 2%

profile of v1, /device:TPU:0, one launch (start us, length us, event | category | flops | bytes accessed | tf_op | source)
XLA Modules:
  0.0 40.9 jit_solution(9953019913968674212)
XLA Ops:
  0.6 0.0 copy-start.2
  0.6 0.0 copy-start.7
  0.7 0.7 %copy-done.2 = s32[1,16,8]{1,2,0:T(8,128)S(1)} copy-done((s32[1,16,8]{1,2,0:T(8,128)S(1)}, s32[1,16,8]{1,2,0:T(8,128)}, u32[]{:S(2)}) %copy-start.2) | copy-done | bytes 536
  1.3 0.0 copy-done.7
  1.3 0.0 copy-start
  1.3 0.9 %copy-done = bf16[128,8,128]{2,1,0:T(8,128)(2,1)S(1)} copy-done((bf16[128,8,128]{2,1,0:T(8,128)(2,1)S(1)}, bf16[128,8,128]{2,1,0:T(8,128)(2,1)}, u32[]{:S(2)}) %copy-start) | copy-done | bytes 262168
  2.3 0.0 copy-start.3
  2.3 0.7 %copy-done.3 = s32[128,8]{0,1:T(8,128)S(1)} copy-done((s32[128,8]{0,1:T(8,128)S(1)}, s32[128,8]{0,1:T(8,128)}, u32[]{:S(2)}) %copy-start.3) | copy-done | bytes 4120
  3.0 0.0 copy-start.4
  3.0 0.7 %copy-done.4 = f32[128,8]{0,1:T(8,128)S(1)} copy-done((f32[128,8]{0,1:T(8,128)S(1)}, f32[128,8]{0,1:T(8,128)}, u32[]{:S(2)}) %copy-start.4) | copy-done | bytes 4120
  3.6 0.0 copy-start.5
  3.6 0.7 %copy-done.5 = f32[8,128]{1,0:T(8,128)S(1)} copy-done((f32[8,128]{1,0:T(8,128)S(1)}, f32[8,128]{1,0:T(8,128)}, u32[]{:S(2)}) %copy-start.5) | copy-done | bytes 4120
  4.3 1.0 %shard_map.95 = (bf16[16,96,128]{2,1,0:T(8,128)(2,1)S(1)}, f32[24,128]{1,0:T(8,128)S(1)}) custom-call(s32[8,16]{1,0:T(8,128)S(1)} %bitcast.10, bf16[128,8,128]{2,1,0:T(8,128)(2,1)S(1)} %copy-done, s32[1,128]{1,0:T(1,128)S(1)} %bitcast.14, s32[8,128]{1,0:T(8,128)S(1)} %bitcast.11, f32[8,128]{1,0:T(8,128)S(1)} %bitcast.12, f32[8,128]{1,0:T(8,128)S(1)} %copy-done.5), custom_call_target="tpu_custom_call" | custom-call | tf_op jit(solution)/shard_map/pallas_call | solution.py:301
  5.3 0.0 copy-start.1
  5.3 19.5 %all_to_all.10.recv_ref = bf16[16,96,128]{2,1,0:T(8,128)(2,1)S(1)} all-to-all(bf16[16,96,128]{2,1,0:T(8,128)(2,1)S(1)} %get-tuple-element.14), channel_id=1, replica_groups=mesh['tile'=16,'tm'=2] {'tile'}, dimensions={0} | all-to-all | bytes 786432 | tf_op jit(solution)/shard_map/all_to_all | solution.py:306
  24.8 0.0 copy-start.6
  24.8 0.0 copy-done.1
  24.8 0.7 %copy-done.6 = s32[128,8]{0,1:T(8,128)S(1)} copy-done((s32[128,8]{0,1:T(8,128)S(1)}, s32[128,8]{0,1:T(8,128)}, u32[]{:S(2)}) %copy-start.6) | copy-done | bytes 4120
  25.5 2.1 %shard_map.96 = (f32[32,8,128]{2,1,0:T(8,128)}, f32[8,128]{1,0:T(8,128)S(1)}, bf16[384,128]{1,0:T(8,128)(2,1)S(1)}, bf16[384,128]{1,0:T(8,128)(2,1)S(1)}) custom-call(bf16[16,96,128]{2,1,0:T(8,128)(2,1)S(1)} %all_to_all.10.recv_ref, bf16[1024,128]{1,0:T(8,128)(2,1)S(1)} %bitcast.9, s32[8,128]{1,0:T(8,128)S(1)} %bitcast.13, ...), custom_call_target="tpu_custom_call" | custom-call | tf_op jit(solution)/shard_map/pallas_call | solution.py:307
  27.6 3.5 %all-to-all-start.1 = ((f32[32,8,128]{2,1,0:T(8,128)}), f32[32,8,128]{2,1,0:T(8,128)S(1)}, u32[]{:S(2)}, u32[]{:S(2)}) async-start(f32[32,8,128]{2,1,0:T(8,128)} %get-tuple-element.16), calls=%async_computation.1 | async-start | bytes 262144 | tf_op jit(solution)/shard_map/all_to_all | solution.py:312
  31.1 0.9 %shard_map.97 = (bf16[384,256]{1,0:T(8,128)(2,1)S(1)}, bf16[384,256]{1,0:T(8,128)(2,1)S(1)}, bf16[512,128]{1,0:T(8,128)(2,1)S(1)}, bf16[512,128]{1,0:T(8,128)(2,1)S(1)}) custom-call(bf16[16,96,128]{2,1,0:T(8,128)(2,1)S(1)} %all_to_all.10.recv_ref), custom_call_target="tpu_custom_call" | custom-call | tf_op jit(solution)/shard_map/pallas_call | solution.py:313
  31.9 7.7 %all-to-all-done.1.recv_ref = f32[32,8,128]{2,1,0:T(8,128)S(1)} async-done(((f32[32,8,128]{2,1,0:T(8,128)}), f32[32,8,128]{2,1,0:T(8,128)S(1)}, u32[]{:S(2)}, u32[]{:S(2)}) %all-to-all-start.1) | async-done | bytes 131104 | tf_op jit(solution)/shard_map/all_to_all | solution.py:312
  39.7 1.2 %shard_map.98 = (f32[8,128]{1,0:T(8,128)}, f32[1,128]{1,0:T(1,128)}) custom-call(f32[32,8,128]{2,1,0:T(8,128)S(1)} %all-to-all-done.1.recv_ref, f32[8,128]{1,0:T(8,128)S(1)} %get-tuple-element.17.sg_ref, f32[24,128]{1,0:T(8,128)S(1)} %get-tuple-element.15.own_ref, bf16[384,256]{1,0:T(8,128)(2,1)S(1)} %get-tuple-element.18.a1h_ref, ...), custom_call_target="tpu_custom_call" | custom-call | tf_op jit(solution)/shard_map/pallas_call | solution.py:318
Async XLA Ops:
  0.6 0.7 %copy-start.2 = (s32[1,16,8]{1,2,0:T(8,128)S(1)}, s32[1,16,8]{1,2,0:T(8,128)}, u32[]{:S(2)}) copy-start(s32[1,16,8]{1,2,0:T(8,128)} %param.9) | copy-start | bytes 1540
  0.6 0.7 %copy-start.7 = (s32[128]{0:T(128)S(1)}, s32[128]{0:T(128)}, u32[]{:S(2)}) copy-start(s32[128]{0:T(128)} %param.12) | copy-start | bytes 1540
  1.3 1.0 %copy-start = (bf16[128,8,128]{2,1,0:T(8,128)(2,1)S(1)}, bf16[128,8,128]{2,1,0:T(8,128)(2,1)}, u32[]{:S(2)}) copy-start(bf16[128,8,128]{2,1,0:T(8,128)(2,1)} %data_ref.1) | copy-start | bytes 786436
  2.3 0.7 %copy-start.3 = (s32[128,8]{0,1:T(8,128)S(1)}, s32[128,8]{0,1:T(8,128)}, u32[]{:S(2)}) copy-start(s32[128,8]{0,1:T(8,128)} %param.13) | copy-start | bytes 12292
  3.0 0.7 %copy-start.4 = (f32[128,8]{0,1:T(8,128)S(1)}, f32[128,8]{0,1:T(8,128)}, u32[]{:S(2)}) copy-start(f32[128,8]{0,1:T(8,128)} %param.14) | copy-start | bytes 12292
  3.6 0.7 %copy-start.5 = (f32[8,128]{1,0:T(8,128)S(1)}, f32[8,128]{1,0:T(8,128)}, u32[]{:S(2)}) copy-start(f32[8,128]{1,0:T(8,128)} %init_ref.1) | copy-start | bytes 12292
  5.3 19.5 %copy-start.1 = (bf16[128,8,128]{2,1,0:T(8,128)(2,1)S(1)}, bf16[128,8,128]{2,1,0:T(8,128)(2,1)}, u32[]{:S(2)}) copy-start(bf16[128,8,128]{2,1,0:T(8,128)(2,1)} %param.11) | copy-start | bytes 786436
  24.8 0.7 %copy-start.6 = (s32[128,8]{0,1:T(8,128)S(1)}, s32[128,8]{0,1:T(8,128)}, u32[]{:S(2)}) copy-start(s32[128,8]{0,1:T(8,128)} %param.10) | copy-start | bytes 12292
  27.6 12.1 %all-to-all-start.1 = ((f32[32,8,128]{2,1,0:T(8,128)}), f32[32,8,128]{2,1,0:T(8,128)S(1)}, u32[]{:S(2)}, u32[]{:S(2)}) async-start(f32[32,8,128]{2,1,0:T(8,128)} %get-tuple-element.16), calls=%async_computation.1 | async-start | bytes 262144 | tf_op jit(solution)/shard_map/all_to_all | solution.py:312

commit v2 on v1

--- a/solution.py
+++ b/solution.py
@@ -18,6 +18,7 @@
 DATA_ROWS = 64
 META_ROWS = 32
 VMEM_LIMIT = 48 * 2 ** 20
+PACK_LIMIT = 60 * 10 ** 6
 NT = (((1,), (1,)), ((), ()))
 
 
@@ -78,10 +79,18 @@
     return rank + (colour_row * QUARTER).astype(jnp.float32)
 
 
-def pack_kernel(n, send_ref, data_ref, colour_ref, corr_ref, gram_ref, init_ref, out_ref, own_ref):
+def pack_kernel(n, *refs):
+    sources, (out_ref, own_ref), held, sems = refs[:7], refs[7:9], refs[9:16], refs[16]
+    send_ref, data_ref, colour_ref, corr_ref, gram_ref, init_ref, slot_ref = held
+    copies = [pltpu.make_async_copy(a, b, sems.at[i]) for i, (a, b) in enumerate(zip(sources, held))]
+    for copy in copies:
+        copy.start()
     me = lax.axis_index("tile")
     lane = iota((8, LANES), 1)
     row = iota((8, LANES), 0)
+    for copy in copies[2:]:
+        copy.wait()
+    own_ref[24:32, :] = slot_ref[...].astype(jnp.float32)
     pos = places(colour_ref[...])
     order = (iota((LANES, LANES), 0).astype(jnp.float32) == pos).astype(jnp.bfloat16)
     ids = corr_ref[...]
@@ -100,6 +109,8 @@
     named = jnp.where(row == 0, pltpu.roll(ident, 64, 1), ident)
     second = jnp.where(lane < 64, pltpu.roll(gram_lo, 96, 1), named)
     meta = jnp.concatenate([first, second, init_hi, init_lo], axis=0).astype(jnp.bfloat16)
+    for copy in copies[:2]:
+        copy.wait()
     for target in range(n):
         out_ref[target, DATA_ROWS:, :] = meta
         blocks = [data_ref[send_ref[c, target]].astype(jnp.float32) for c in range(8)]
@@ -122,21 +133,21 @@
     return total
 
 
-def project_kernel(n, tm, recv_ref, fp_ref, slot_ref, own_ref, out_ref, sg_ref, a3h_ref, a3l_ref):
+def project_kernel(n, tm, recv_ref, fp_ref, own_ref, out_ref, sg_ref, a3h_ref, a3l_ref):
     me = lax.axis_index("tile")
     lane = iota((8, LANES), 1)
     row = iota((8, LANES), 0)
     wide = 8 * LANES
     widen = (lax.shift_right_logical(iota((LANES, wide), 1), 3) == iota((LANES, wide), 0)).astype(jnp.bfloat16)
-    narrow = jnp.concatenate([slot_ref[...].astype(jnp.float32), own_ref[16:24, :]], axis=0)
+    narrow = own_ref[16:32, :]
     if n * 8 <= 256:
         wider = dot(narrow.astype(jnp.bfloat16), widen)
     else:
         wider = join3(dot(split3(narrow), widen))
     mine = jnp.bitwise_and(iota((8, wide), 1), 7) == iota((8, wide), 0)
-    slot_row = jnp.sum(jnp.where(mine, wider[0:8], 0.0), axis=0, keepdims=True)
+    slot_row = jnp.sum(jnp.where(mine, wider[8:16], 0.0), axis=0, keepdims=True)
     slot_row = jnp.broadcast_to(slot_row, (8, wide))
-    order = (iota((LANES, wide), 0).astype(jnp.float32) == wider[8:9]).astype(jnp.bfloat16)
+    order = (iota((LANES, wide), 0).astype(jnp.float32) == wider[0:1]).astype(jnp.bfloat16)
     weights = fp_ref[...]
     total = jnp.zeros((8, wide), jnp.float32)
     group = 4
@@ -289,26 +300,38 @@
     tm = lax.axis_size("tm")
     f32, bf16 = jnp.float32, jnp.bfloat16
     shape = jax.ShapeDtypeStruct
-    params = pltpu.CompilerParams(vmem_limit_bytes=VMEM_LIMIT)
     vmem = pl.BlockSpec(memory_space=pltpu.VMEM)
-    smem = pl.BlockSpec(memory_space=pltpu.SMEM)
-
-    def call(body, outs, ins):
+    hbm = pl.BlockSpec(memory_space=pltpu.HBM)
+
+    def call(body, outs, ins, scratch=(), limit=VMEM_LIMIT):
         return pl.pallas_call(
-            body, out_shape=outs, in_specs=ins, out_specs=[vmem] * len(outs), compiler_params=params
+            body,
+            out_shape=outs,
+            in_specs=ins,
+            out_specs=[vmem] * len(outs),
+            scratch_shapes=scratch,
+            compiler_params=pltpu.CompilerParams(vmem_limit_bytes=limit),
         )
 
+    inputs = (
+        send_list[0].T, data, colour.reshape(1, LANES), correlation.T, correlation_gram.T, traces_init,
+        footprint_slot.T,
+    )
     outgoing, own = call(
         functools.partial(pack_kernel, n),
-        [shape((n, DATA_ROWS + META_ROWS, LANES), bf16), shape((24, LANES), f32)],
-        [smem] + [vmem] * 5,
-    )(send_list[0].T, data, colour.reshape(1, LANES), correlation.T, correlation_gram.T, traces_init)
+        [shape((n, DATA_ROWS + META_ROWS, LANES), bf16), shape((32, LANES), f32)],
+        [hbm] * 7,
+        [pltpu.SMEM(inputs[0].shape, jnp.int32)]
+        + [pltpu.VMEM(x.shape, x.dtype) for x in inputs[1:]]
+        + [pltpu.SemaphoreType.DMA((7,))],
+        PACK_LIMIT,
+    )(*inputs)
     arrived = lax.all_to_all(outgoing, "tile", split_axis=0, concat_axis=0, tiled=True)
     message, self_gram, a3h, a3l = call(
         functools.partial(project_kernel, n, tm),
         [shape((n * tm, 8, LANES), f32), shape((8, LANES), f32)] + [shape((384, LANES), bf16)] * 2,
-        [vmem] * 4,
-    )(arrived, footprint.reshape(8 * LANES, LANES), footprint_slot.T, own)
+        [vmem] * 3,
+    )(arrived, footprint.reshape(8 * LANES, LANES), own)
     messages = lax.all_to_all(message, ("tile", "tm"), split_axis=0, concat_axis=0, tiled=True)
     a1h, a1l, a2h, a2l = call(
         functools.partial(coef_kernel, n),

time: 41.3 us -> 38.2 us (0.925)
  local copies, waits for them, and re-layouts: 4.37 us -> 0.01 us
  Pallas kernels: 5.18 us -> 6.32 us
    unnamed x16 -> x4, local copies, waits for them, and re-layouts: 4.37 us -> 0.01 us
    pallas_call x1, Pallas kernels: 0.99 us -> 2.13 us  [shards(): call(functools.partial(pack_kernel, n), [shape((n, DATA_ROWS + META_ROWS,...]
where the time goes in v2:
time: 38.2 us; the launch traced here: 37.9 us
  blocking collectives  19.7 us (52%)
  waiting for transfers between devices  7.73 us (20%)
  Pallas kernels  6.32 us (17%)
  starting transfers between devices  3.46 us (9%)
  between operations  0.67 us (2%)
    all_to_all x1, blocking collectives, shards(): lax.all_to_all(outgoing, 'tile', split_axis=0, concat_axis=0, tiled=True)  19.7 us
    all_to_all x1, waiting for transfers between devices, shards(): lax.all_to_all(message, ('tile', 'tm'), split_axis=0, concat_axis=0, tile...  7.73 us
    all_to_all x1, starting transfers between devices, shards(): lax.all_to_all(message, ('tile', 'tm'), split_axis=0, concat_axis=0, tile...  3.46 us
    pallas_call x1, Pallas kernels, shards(): call(functools.partial(pack_kernel, n), [shape((n, DATA_ROWS + META_ROWS,...  2.13 us
    pallas_call x1, Pallas kernels, shards(): call(functools.partial(project_kernel, n, tm), [shape((n * tm, 8, LANES),...  2.06 us
    pallas_call x1, Pallas kernels, shards(): call(functools.partial(sweep_kernel, n, tm), [shape((8, LANES), f32), sha...  1.24 us
    pallas_call x1, Pallas kernels, shards(): call(functools.partial(coef_kernel, n), [shape((384, 2 * LANES), bf16)] *...  0.89 us
  transfers between devices with their start and end apart: 1, of which 1 were waited for; matrix products, arithmetic and copies ran while one was open for 0% of the time, Pallas kernels for 2%

profile of v2, /device:TPU:0, one launch (start us, length us, event | category | flops | bytes accessed | tf_op | source)
XLA Modules:
  0.0 37.9 jit_solution(10910457958844493039)
XLA Ops:
  0.6 2.1 %shard_map.95 = (bf16[16,96,128]{2,1,0:T(8,128)(2,1)}, f32[32,128]{1,0:T(8,128)}) custom-call(s32[8,16]{1,0:T(8,128)} %bitcast.10, bf16[128,8,128]{2,1,0:T(8,128)(2,1)} %refs_1_.1, s32[1,128]{1,0:T(1,128)} %bitcast.14, s32[8,128]{1,0:T(8,128)} %bitcast.11, f32[8,128]{1,0:T(8,128)} %bitcast.12, f32[8,128]{1,0:T(8,128)} %refs_5_.1, s32[8,128]{1,0:T(8,128)} %bitcast.13), custom_call_target="tpu_custom_call" | custom-call | tf_op jit(solution)/shard_map/pallas_call | solution.py:320
  2.8 0.0 copy-start
  2.8 0.0 copy-start.1
  2.8 19.7 %all_to_all.10.recv_ref = bf16[16,96,128]{2,1,0:T(8,128)(2,1)S(1)} all-to-all(bf16[16,96,128]{2,1,0:T(8,128)(2,1)} %get-tuple-element.14), channel_id=1, replica_groups=mesh['tile'=16,'tm'=2] {'tile'}, dimensions={0} | all-to-all | bytes 786432 | tf_op jit(solution)/shard_map/all_to_all | solution.py:329
  22.5 0.0 copy-done
  22.5 0.0 copy-done.1
  22.5 2.1 %shard_map.96 = (f32[32,8,128]{2,1,0:T(8,128)}, f32[8,128]{1,0:T(8,128)S(1)}, bf16[384,128]{1,0:T(8,128)(2,1)S(1)}, bf16[384,128]{1,0:T(8,128)(2,1)S(1)}) custom-call(bf16[16,96,128]{2,1,0:T(8,128)(2,1)S(1)} %all_to_all.10.recv_ref, bf16[1024,128]{1,0:T(8,128)(2,1)S(1)} %bitcast.9, f32[32,128]{1,0:T(8,128)S(1)} %copy-done.1), custom_call_target="tpu_custom_call" | custom-call | tf_op jit(solution)/shard_map/pallas_call | solution.py:330
  24.6 3.5 %all-to-all-start.1 = ((f32[32,8,128]{2,1,0:T(8,128)}), f32[32,8,128]{2,1,0:T(8,128)S(1)}, u32[]{:S(2)}, u32[]{:S(2)}) async-start(f32[32,8,128]{2,1,0:T(8,128)} %get-tuple-element.16), calls=%async_computation.1 | async-start | bytes 262144 | tf_op jit(solution)/shard_map/all_to_all | solution.py:335
  28.0 0.9 %shard_map.97 = (bf16[384,256]{1,0:T(8,128)(2,1)S(1)}, bf16[384,256]{1,0:T(8,128)(2,1)S(1)}, bf16[512,128]{1,0:T(8,128)(2,1)S(1)}, bf16[512,128]{1,0:T(8,128)(2,1)S(1)}) custom-call(bf16[16,96,128]{2,1,0:T(8,128)(2,1)S(1)} %all_to_all.10.recv_ref), custom_call_target="tpu_custom_call" | custom-call | tf_op jit(solution)/shard_map/pallas_call | solution.py:336
  28.9 7.7 %all-to-all-done.1.recv_ref = f32[32,8,128]{2,1,0:T(8,128)S(1)} async-done(((f32[32,8,128]{2,1,0:T(8,128)}), f32[32,8,128]{2,1,0:T(8,128)S(1)}, u32[]{:S(2)}, u32[]{:S(2)}) %all-to-all-start.1) | async-done | bytes 131104 | tf_op jit(solution)/shard_map/all_to_all | solution.py:335
  36.7 1.2 %shard_map.98 = (f32[8,128]{1,0:T(8,128)}, f32[1,128]{1,0:T(1,128)}) custom-call(f32[32,8,128]{2,1,0:T(8,128)S(1)} %all-to-all-done.1.recv_ref, f32[8,128]{1,0:T(8,128)S(1)} %get-tuple-element.17.sg_ref, f32[32,128]{1,0:T(8,128)S(1)} %copy-done.1, bf16[384,256]{1,0:T(8,128)(2,1)S(1)} %get-tuple-element.18.a1h_ref, ...), custom_call_target="tpu_custom_call" | custom-call | tf_op jit(solution)/shard_map/pallas_call | solution.py:341
Async XLA Ops:
  2.8 19.7 %copy-start = (bf16[128,8,128]{2,1,0:T(8,128)(2,1)S(1)}, bf16[128,8,128]{2,1,0:T(8,128)(2,1)}, u32[]{:S(2)}) copy-start(bf16[128,8,128]{2,1,0:T(8,128)(2,1)} %param.11) | copy-start | bytes 786436
  2.8 19.7 %copy-start.1 = (f32[32,128]{1,0:T(8,128)S(1)}, f32[32,128]{1,0:T(8,128)}, u32[]{:S(2)}) copy-start(f32[32,128]{1,0:T(8,128)} %get-tuple-element.15.own_ref) | copy-start | bytes 49156
  24.6 12.1 %all-to-all-start.1 = ((f32[32,8,128]{2,1,0:T(8,128)}), f32[32,8,128]{2,1,0:T(8,128)S(1)}, u32[]{:S(2)}, u32[]{:S(2)}) async-start(f32[32,8,128]{2,1,0:T(8,128)} %get-tuple-element.16), calls=%async_computation.1 | async-start | bytes 262144 | tf_op jit(solution)/shard_map/all_to_all | solution.py:335

commit v3 on v2

--- a/solution.py
+++ b/solution.py
@@ -18,7 +18,7 @@
 DATA_ROWS = 64
 META_ROWS = 32
 VMEM_LIMIT = 48 * 2 ** 20
-PACK_LIMIT = 60 * 10 ** 6
+PACK_LIMIT = 48 * 2 ** 20
 NT = (((1,), (1,)), ((), ()))
 
 
@@ -325,7 +325,7 @@
         + [pltpu.VMEM(x.shape, x.dtype) for x in inputs[1:]]
         + [pltpu.SemaphoreType.DMA((7,))],
         PACK_LIMIT,
-    )(*inputs)
+    )(*[pltpu.with_memory_space_constraint(x, pltpu.HBM) for x in inputs])
     arrived = lax.all_to_all(outgoing, "tile", split_axis=0, concat_axis=0, tiled=True)
     message, self_gram, a3h, a3l = call(
         functools.partial(project_kernel, n, tm),

time: 38.2 us -> 37.1 us (0.971)
  Pallas kernels: 6.32 us -> 5.56 us
    pallas_call x1, Pallas kernels: 2.13 us -> 1.37 us  [shards(): call(functools.partial(pack_kernel, n), [shape((n, DATA_ROWS + META_ROWS,...]
where the time goes in v3:
time: 37.1 us; the launch traced here: 36.9 us
  blocking collectives  19.5 us (53%)
  waiting for transfers between devices  7.73 us (21%)
  Pallas kernels  5.56 us (15%)
  starting transfers between devices  3.46 us (9%)
  between operations  0.66 us (2%)
    all_to_all x1, blocking collectives, shards(): lax.all_to_all(outgoing, 'tile', split_axis=0, concat_axis=0, tiled=True)  19.5 us
    all_to_all x1, waiting for transfers between devices, shards(): lax.all_to_all(message, ('tile', 'tm'), split_axis=0, concat_axis=0, tile...  7.73 us
    all_to_all x1, starting transfers between devices, shards(): lax.all_to_all(message, ('tile', 'tm'), split_axis=0, concat_axis=0, tile...  3.46 us
    pallas_call x1, Pallas kernels, shards(): call(functools.partial(project_kernel, n, tm), [shape((n * tm, 8, LANES),...  2.05 us
    pallas_call x1, Pallas kernels, shards(): call(functools.partial(pack_kernel, n), [shape((n, DATA_ROWS + META_ROWS,...  1.37 us
    pallas_call x1, Pallas kernels, shards(): call(functools.partial(sweep_kernel, n, tm), [shape((8, LANES), f32), sha...  1.24 us
    pallas_call x1, Pallas kernels, shards(): call(functools.partial(coef_kernel, n), [shape((384, 2 * LANES), bf16)] *...  0.89 us
  transfers between devices with their start and end apart: 1, of which 1 were waited for; matrix products, arithmetic and copies ran while one was open for 0% of the time, Pallas kernels for 2%

profile of v3, /device:TPU:0, one launch (start us, length us, event | category | flops | bytes accessed | tf_op | source)
XLA Modules:
  0.0 36.9 jit_solution(18037740319714552723)
XLA Ops:
  0.6 1.4 %shard_map.95 = (bf16[16,96,128]{2,1,0:T(8,128)(2,1)S(1)}, f32[32,128]{1,0:T(8,128)S(1)}) custom-call(s32[8,16]{1,0:T(8,128)} %bitcast.10, bf16[128,8,128]{2,1,0:T(8,128)(2,1)} %refs_1_.1, s32[1,128]{1,0:T(1,128)} %bitcast.14, s32[8,128]{1,0:T(8,128)} %bitcast.11, f32[8,128]{1,0:T(8,128)} %bitcast.12, f32[8,128]{1,0:T(8,128)} %refs_5_.1, s32[8,128]{1,0:T(8,128)} %bitcast.13), custom_call_target="tpu_custom_call" | custom-call | tf_op jit(solution)/shard_map/pallas_call | solution.py:320
  2.0 0.0 copy-start
  2.0 19.5 %all_to_all.10.recv_ref = bf16[16,96,128]{2,1,0:T(8,128)(2,1)S(1)} all-to-all(bf16[16,96,128]{2,1,0:T(8,128)(2,1)S(1)} %get-tuple-element.14), channel_id=1, replica_groups=mesh['tile'=16,'tm'=2] {'tile'}, dimensions={0} | all-to-all | bytes 786432 | tf_op jit(solution)/shard_map/all_to_all | solution.py:329
  21.5 0.0 copy-done
  21.5 2.1 %shard_map.96 = (f32[32,8,128]{2,1,0:T(8,128)}, f32[8,128]{1,0:T(8,128)S(1)}, bf16[384,128]{1,0:T(8,128)(2,1)S(1)}, bf16[384,128]{1,0:T(8,128)(2,1)S(1)}) custom-call(bf16[16,96,128]{2,1,0:T(8,128)(2,1)S(1)} %all_to_all.10.recv_ref, bf16[1024,128]{1,0:T(8,128)(2,1)S(1)} %bitcast.9, f32[32,128]{1,0:T(8,128)S(1)} %get-tuple-element.15.own_ref), custom_call_target="tpu_custom_call" | custom-call | tf_op jit(solution)/shard_map/pallas_call | solution.py:330
  23.6 3.5 %all-to-all-start.1 = ((f32[32,8,128]{2,1,0:T(8,128)}), f32[32,8,128]{2,1,0:T(8,128)S(1)}, u32[]{:S(2)}, u32[]{:S(2)}) async-start(f32[32,8,128]{2,1,0:T(8,128)} %get-tuple-element.16), calls=%async_computation.1 | async-start | bytes 262144 | tf_op jit(solution)/shard_map/all_to_all | solution.py:335
  27.0 0.9 %shard_map.97 = (bf16[384,256]{1,0:T(8,128)(2,1)S(1)}, bf16[384,256]{1,0:T(8,128)(2,1)S(1)}, bf16[512,128]{1,0:T(8,128)(2,1)S(1)}, bf16[512,128]{1,0:T(8,128)(2,1)S(1)}) custom-call(bf16[16,96,128]{2,1,0:T(8,128)(2,1)S(1)} %all_to_all.10.recv_ref), custom_call_target="tpu_custom_call" | custom-call | tf_op jit(solution)/shard_map/pallas_call | solution.py:336
  27.9 7.7 %all-to-all-done.1.recv_ref = f32[32,8,128]{2,1,0:T(8,128)S(1)} async-done(((f32[32,8,128]{2,1,0:T(8,128)}), f32[32,8,128]{2,1,0:T(8,128)S(1)}, u32[]{:S(2)}, u32[]{:S(2)}) %all-to-all-start.1) | async-done | bytes 131104 | tf_op jit(solution)/shard_map/all_to_all | solution.py:335
  35.7 1.2 %shard_map.98 = (f32[8,128]{1,0:T(8,128)}, f32[1,128]{1,0:T(1,128)}) custom-call(f32[32,8,128]{2,1,0:T(8,128)S(1)} %all-to-all-done.1.recv_ref, f32[8,128]{1,0:T(8,128)S(1)} %get-tuple-element.17.sg_ref, f32[32,128]{1,0:T(8,128)S(1)} %get-tuple-element.15.own_ref, bf16[384,256]{1,0:T(8,128)(2,1)S(1)} %get-tuple-element.18.a1h_ref, ...), custom_call_target="tpu_custom_call" | custom-call | tf_op jit(solution)/shard_map/pallas_call | solution.py:341
Async XLA Ops:
  2.0 19.5 %copy-start = (bf16[128,8,128]{2,1,0:T(8,128)(2,1)S(1)}, bf16[128,8,128]{2,1,0:T(8,128)(2,1)}, u32[]{:S(2)}) copy-start(bf16[128,8,128]{2,1,0:T(8,128)(2,1)} %param.11) | copy-start | bytes 786436
  23.6 12.1 %all-to-all-start.1 = ((f32[32,8,128]{2,1,0:T(8,128)}), f32[32,8,128]{2,1,0:T(8,128)S(1)}, u32[]{:S(2)}, u32[]{:S(2)}) async-start(f32[32,8,128]{2,1,0:T(8,128)} %get-tuple-element.16), calls=%async_computation.1 | async-start | bytes 262144 | tf_op jit(solution)/shard_map/all_to_all | solution.py:335

commit v4 on v3

v4 whole, which is shorter than its diff:
```python
import functools

import jax
import jax.numpy as jnp
from jax import lax
from jax.experimental import pallas as pl
from jax.experimental.pallas import tpu as pltpu
from jax.sharding import PartitionSpec as P

REACH = (
    (0, 0), (1, 0), (-1, 0), (0, 1),
    (1, 1), (-1, 1), (2, 0), (-2, 0),
    (3, 0), (-3, 0), (2, 1), (-2, 1),
)
NEAR = REACH[:4]
LANES = 128
QUARTER = 32
DATA_ROWS = 64
META_ROWS = 32
GROUP = 4
VMEM_LIMIT = 48 * 2 ** 20
PACK_LIMIT = 48 * 2 ** 20
NT = (((1,), (1,)), ((), ()))


def iota(shape, dim):
    return lax.broadcasted_iota(jnp.int32, shape, dim)


def reach_at(device, near):
    return REACH.index((device[0] + near[0], (device[1] + near[1]) % 2))


def tile_at(me, rel, n):
    return lax.rem(me + rel[0] + rel[1] * (n // 2) + n, n)


def dot(a, b):
    return jnp.dot(a, b, preferred_element_type=jnp.float32)


def dot_nt(a, b):
    return lax.dot_general(a, b, NT, preferred_element_type=jnp.float32)


def split2(x):
    hi = x.astype(jnp.bfloat16).astype(jnp.float32)
    return hi, x - hi


def split3(x):
    hi, rest = split2(x)
    mid, low = split2(rest)
    return jnp.concatenate([hi, mid, low], axis=0).astype(jnp.bfloat16)


def places(colour_row):
    in_class = colour_row == iota((8, LANES), 0)
    before = (iota((LANES, LANES), 0) < iota((LANES, LANES), 1)).astype(jnp.bfloat16)
    counts = dot(in_class.astype(jnp.bfloat16), before)
    rank = jnp.sum(jnp.where(in_class, counts, 0.0), axis=0, keepdims=True)
    return rank + (colour_row * QUARTER).astype(jnp.float32)


def pack_kernel(n, *refs):
    sources, (out_ref, own_ref), held, sems = refs[:7], refs[7:9], refs[9:16], refs[16]
    send_ref, data_ref, colour_ref, corr_ref, gram_ref, init_ref, slot_ref = held
    copies = [pltpu.make_async_copy(a, b, sems.at[i]) for i, (a, b) in enumerate(zip(sources, held))]
    for copy in copies:
        copy.start()
    me = lax.axis_index("tile")
    lane = iota((8, LANES), 1)
    row = iota((8, LANES), 0)
    for copy in copies[2:]:
        copy.wait()
    own_ref[24:32, :] = slot_ref[...].astype(jnp.float32)
    pos = places(colour_ref[...])
    order = (iota((LANES, LANES), 0).astype(jnp.float32) == pos).astype(jnp.bfloat16)
    ids = corr_ref[...]
    away = jnp.bitwise_and(lax.shift_right_logical(ids, 7) - me, n - 1)
    which = jnp.where(away == 0, 0, jnp.where(away == 1, 1, jnp.where(away == n - 1, 2, 3)))
    code = which * LANES + jnp.bitwise_and(ids, LANES - 1) - 2 * LANES
    code = code.astype(jnp.float32)
    gram = gram_ref[...]
    gram_hi, gram_lo = split2(gram)
    init_hi, init_lo = split2(init_ref[...])
    rows = [code, gram_hi, gram_lo, lane.astype(jnp.float32)]
    placed = dot_nt(jnp.concatenate(rows, axis=0).astype(jnp.bfloat16), order)
    own_ref[0:8, :] = code
    own_ref[8:16, :] = gram
    own_ref[16:24, :] = jnp.broadcast_to(pos, (8, LANES))
    own_ref[32:40, :] = placed[24:32]
    first = jnp.where(lane < 64, pltpu.roll(placed[0:8], 96, 1), pltpu.roll(placed[8:16], 32, 1))
    spread = jnp.where(row == 0, pltpu.roll(jnp.broadcast_to(pos, (8, LANES)), 64, 1), pos)
    second = jnp.where(lane < 64, pltpu.roll(placed[16:24], 96, 1), spread)
    meta = jnp.concatenate([first, second, init_hi, init_lo], axis=0).astype(jnp.bfloat16)
    for copy in copies[:2]:
        copy.wait()
    for target in range(n):
        out_ref[target, DATA_ROWS:, :] = meta
        blocks = [data_ref[send_ref[c, target]].astype(jnp.float32) for c in range(8)]
        out_ref[target, :DATA_ROWS, :] = jnp.concatenate(blocks, axis=0).astype(jnp.bfloat16)


def lookup(table, index):
    return jnp.take_along_axis(table, index, axis=1)


def spread_row(rows, i):
    return jnp.broadcast_to(rows[i : i + 1], (8, LANES))


def pick(cases, which):
    out = cases[-1]
    for i in range(len(cases) - 1):
        out = jnp.where(which == i, cases[i], out)
    return out


def edges(devices, places_of, which, index, weight, sources):
    place, device = None, None
    for f in devices:
        found = lookup(places_of[f], index)
        place = found if place is None else jnp.where(which == f, found, place)
    place = place.astype(jnp.int32)
    colour = lax.shift_right_logical(place, 5)
    turn = jnp.bitwise_and(which + colour, 3)
    lanes = turn * QUARTER + jnp.bitwise_and(place, QUARTER - 1)
    tile = colour * 4 + lax.shift_right_logical(which, 2)
    return lanes, [jnp.where(tile == c * 4 + g, weight, 0.0) for c, g in sources]


SOURCES = (
    ((0, 0), (0, 1)),
    ((0, 0), (0, 1), (0, 2)),
    ((0, 0), (0, 1), (1, 0), (1, 1)),
    ((0, 0), (1, 0), (2, 0)),
)


def project_kernel(n, tm, recv_ref, fp_ref, own_ref, out_ref, gram_ref, lanes_ref, weights_ref, wide_ref):
    me = lax.axis_index("tile")
    lane = iota((8, LANES), 1)
    row = iota((8, LANES), 0)
    wide_ref[...] = fp_ref[...].astype(jnp.float32)
    weights, squares = [], None
    for j in range(8):
        rows = wide_ref[pl.ds(j, LANES, stride=8), :]
        weights.append(rows.astype(jnp.bfloat16))
        squares = rows * rows if j == 0 else squares + rows * rows
    weights = jnp.concatenate(weights, axis=0)
    gram = dot_nt(jnp.ones((8, LANES), jnp.bfloat16), split3(squares))
    gram = gram[:, :LANES] + gram[:, LANES : 2 * LANES] + gram[:, 2 * LANES :]
    slot_row = jnp.concatenate([own_ref[24 + j : 25 + j, :] for j in range(8)], axis=1)
    slot_row = jnp.broadcast_to(slot_row, (8, 8 * LANES))
    total = jnp.zeros((8, 8 * LANES), jnp.float32)
    for source in range(0, n, GROUP):
        blocks = recv_ref[source : source + GROUP, :DATA_ROWS, :].reshape(GROUP * DATA_ROWS, LANES)
        product = dot_nt(blocks, weights)
        for c in range(GROUP * 8):
            hit = slot_row == float(source * 8 + c)
            total = jnp.where(hit, product[8 * c : 8 * c + 8], total)
    projected = total[:, :LANES]
    for j in range(1, 8):
        projected = projected + total[:, j * LANES : (j + 1) * LANES]
    metas = [recv_ref[tile_at(me, rel, n), DATA_ROWS:, :].astype(jnp.float32) for rel in REACH]
    places_of = []
    for meta in metas:
        found = jnp.where(lane < 64, pltpu.roll(spread_row(meta, 8), 64, 1), spread_row(meta, 9))
        places_of.append(found)
    code = own_ref[0:8, :].astype(jnp.int32) + 2 * LANES
    index, which = jnp.bitwise_and(code, LANES - 1), lax.shift_right_logical(code, 7)
    place = pick([lookup(places_of[r], index) for r in range(4)], which).astype(jnp.int32)
    own_place = own_ref[16:24, :].astype(jnp.int32)
    after = lax.shift_right_logical(place, 5) > lax.shift_right_logical(own_place, 5)
    late = jnp.where(after, own_ref[8:16, :], 0.0)
    starts = [meta[16:24] + meta[24:32] for meta in metas[:4]]
    held = None
    for i in range(8):
        at, owner = spread_row(index, i), spread_row(which, i)
        term = pick([lookup(start, at) for start in starts], owner) * spread_row(late, i)
        held = term if held is None else held + term
    names = own_ref[32:40, :].astype(jnp.int32)
    base = lookup(projected - held, names)
    gram = lookup(gram, names)
    gram_ref[...] = gram
    message = jnp.where(lane < QUARTER, jnp.maximum(base / gram, 0.0), base)
    grams12 = jnp.where(row == 0, pltpu.roll(gram, 64, 1), pltpu.roll(gram, 32, 1))
    others = jnp.where(lane < 96, message, grams12)
    for t in range(n * tm):
        out_ref[t] = others
    for i, rel in enumerate(REACH):
        source = message if i == 0 else others
        turned = source if i % 4 == 0 else pltpu.roll(source, QUARTER * (i % 4), 1)
        target = tile_at(me, (-rel[0], rel[1]), n)
        for t in range(tm):
            out_ref[target * tm + t] = turned
    block = lax.shift_right_logical(lane, 5)
    codes = []
    for i in range(8):
        code = metas[i][0:8].astype(jnp.int32) + 2 * LANES
        at = [reach_at(REACH[i], near) for near in NEAR]
        device = pick(at, lax.shift_right_logical(code, 7))
        codes.append((device * LANES + jnp.bitwise_and(code, LANES - 1)).astype(jnp.float32))

    def gathered(parts, group, colour, start):
        out = None
        for q in range(4):
            p = (q + colour) % 4
            shift = (QUARTER * p - start) % LANES
            turned = parts[4 * group + q]
            turned = turned if shift == 0 else pltpu.roll(turned, shift, 1)
            out = turned if out is None else jnp.where(block == p, turned, out)
        return out

    hi, low = [meta[0:8] for meta in metas[:8]], [meta[8:16] for meta in metas[:8]]
    slot = 0
    for step, (group, colour) in enumerate(((0, 1), (1, 1), (0, 2), (0, 3))):
        if step < 3:
            start = QUARTER * (colour - 1)
            code = gathered(codes, group, colour, start).astype(jnp.int32)
            weight = gathered(hi, group, colour, start + 64) + gathered(low, group, colour, start)
            device, at = lax.shift_right_logical(code, 7), jnp.bitwise_and(code, LANES - 1)
            devices = range(12) if step == 1 else range(8)
        else:
            weight = lookup(own_ref[8:16, :], names)
            device, at = lookup(which, names), lookup(index, names)
            devices = range(4)
        lanes, parts = edges(devices, places_of, device, at, weight, SOURCES[step])
        lanes_ref[8 * step : 8 * step + 8, :] = lanes
        for part in parts:
            weights_ref[8 * slot : 8 * slot + 8, :] = part
            slot += 1


def sweep_kernel(n, tm, recv_ref, gram_ref, own_ref, lanes_ref, weights_ref, traces_ref, rms_ref):
    me = lax.axis_index("tile")
    half = lax.axis_index("tm")
    lane = iota((8, LANES), 1)
    block = lax.shift_right_logical(lane, 5)
    first = [tile_at(me, rel, n) * tm for rel in REACH]
    gram = gram_ref[...]

    def gathered(messages, group, turn):
        out = messages[4 * group]
        for q in range(4):
            if q or turn:
                out = jnp.where(block == (q + turn) % 4, messages[4 * group + q], out)
        return out

    def gram_of(messages, group, colour):
        rows = spread_row(gathered(messages, group, 3), colour - 1)
        rows = pltpu.roll(rows, 64 if colour == 1 else 96, 1)
        return jnp.where(block == colour, gram, rows) if group == 0 else rows

    def neighbours(step, tiles):
        slot = sum(len(sources) for sources in SOURCES[:step])
        total = None
        for i in range(8):
            at = jnp.broadcast_to(lanes_ref[8 * step + i : 8 * step + i + 1, :], (8, LANES))
            for s, tile in enumerate(tiles):
                place = 8 * (slot + s) + i
                term = lookup(tile, at) * weights_ref[place : place + 1, :]
                total = term if total is None else total + term
        return total

    energy, mine = None, None
    for t in range(tm):
        messages = [recv_ref[f + t] for f in first]
        x0 = [gathered(messages, group, 0) for group in range(3)]
        x1 = []
        for group in range(2):
            fresh = gathered(messages, group, 1) - neighbours(group, x0[: 2 + group])
            x1.append(jnp.maximum(fresh / gram_of(messages, group, 1), 0.0))
        fresh = gathered(messages, 0, 2) - neighbours(2, [x0[0], x0[1], x1[0], x1[1]])
        x2 = jnp.maximum(fresh / gram_of(messages, 0, 2), 0.0)
        fresh = messages[0] - neighbours(3, [x0[0], x1[0], x2])
        x3 = jnp.maximum(fresh / gram, 0.0)
        own = pick([messages[0], x1[0], x2, x3], block)
        square = jnp.sum(own * own, axis=0, keepdims=True)
        energy = square if energy is None else energy + square
        mine = own if mine is None else jnp.where(half == t, own, mine)
    order = own_ref[16:24, :].astype(jnp.int32)
    traces_ref[...] = lookup(mine, order)
    energy = lookup(jnp.broadcast_to(energy, (8, LANES)), order)
    rms_ref[...] = jnp.sqrt(energy[0:1] / (8 * tm) + 1e-06)


def shards(
    data, send_list, footprint_slot, footprint, colour, correlation, correlation_gram, traces_init
):
    n = lax.axis_size("tile")
    tm = lax.axis_size("tm")
    f32, bf16 = jnp.float32, jnp.bfloat16
    shape = jax.ShapeDtypeStruct
    vmem = pl.BlockSpec(memory_space=pltpu.VMEM)
    hbm = pl.BlockSpec(memory_space=pltpu.HBM)

    def call(body, outs, ins, scratch=(), limit=VMEM_LIMIT):
        return pl.pallas_call(
            body,
            out_shape=outs,
            in_specs=ins,
            out_specs=[vmem] * len(outs),
            scratch_shapes=scratch,
            compiler_params=pltpu.CompilerParams(vmem_limit_bytes=limit),
        )

    inputs = (
        send_list[0].T, data, colour.reshape(1, LANES), correlation.T, correlation_gram.T, traces_init,
        footprint_slot.T,
    )
    outgoing, own = call(
        functools.partial(pack_kernel, n),
        [shape((n, DATA_ROWS + META_ROWS, LANES), bf16), shape((40, LANES), f32)],
        [hbm] * 7,
        [pltpu.SMEM(inputs[0].shape, jnp.int32)]
        + [pltpu.VMEM(x.shape, x.dtype) for x in inputs[1:]]
        + [pltpu.SemaphoreType.DMA((7,))],
        PACK_LIMIT,
    )(*[pltpu.with_memory_space_constraint(x, pltpu.HBM) for x in inputs])
    arrived = lax.all_to_all(outgoing, "tile", split_axis=0, concat_axis=0, tiled=True)
    slots = sum(len(sources) for sources in SOURCES)
    message, gram, lanes, weights = call(
        functools.partial(project_kernel, n, tm),
        [shape((n * tm, 8, LANES), f32), shape((8, LANES), f32)]
        + [shape((8 * len(SOURCES), LANES), jnp.int32), shape((8 * slots, LANES), f32)],
        [vmem] * 3,
        [pltpu.VMEM((8 * LANES, LANES), f32)],
    )(arrived, footprint.reshape(8 * LANES, LANES), own)
    messages = lax.all_to_all(message, ("tile", "tm"), split_axis=0, concat_axis=0, tiled=True)
    traces, rms = call(
        functools.partial(sweep_kernel, n, tm),
        [shape((8, LANES), f32), shape((1, LANES), f32)],
        [vmem] * 5,
    )(messages, gram, own, lanes, weights)
    return (traces, rms.reshape(LANES))


def solution(mesh):
    placed = (
        P("tile", "tm", None),
        P("tile", None, None),
        P("tile", None),
        P("tile", None, None),
        P("tile"),
        P("tile", None),
        P("tile", None),
        P("tm", "tile"),
    )
    return jax.shard_map(
        shards, mesh=mesh, in_specs=placed, out_specs=(P("tm", "tile"), P("tile")), check_vma=False
    )
```

time: 37.1 us -> 35.9 us (0.968)
  blocking collectives: 19.5 us -> 31.4 us
  waiting for transfers between devices: 7.73 us -> 0 us
  starting transfers between devices: 3.46 us -> 0 us
  Pallas kernels: 5.56 us -> 3.64 us
    all_to_all x0 -> x1, blocking collectives: none -> 11.9 us  [shards(): lax.all_to_all(message, ('tile', 'tm'), split_axis=0, concat_axis=0, tile...]
    all_to_all x1 -> x0, waiting for transfers between devices: 7.73 us -> none  [shards(): lax.all_to_all(message, ('tile', 'tm'), split_axis=0, concat_axis=0, tile...]
    all_to_all x1 -> x0, starting transfers between devices: 3.46 us -> none  [shards(): lax.all_to_all(message, ('tile', 'tm'), split_axis=0, concat_axis=0, tile...]
    pallas_call x1, Pallas kernels: 2.05 us -> 1 us  [shards(): call(functools.partial(project_kernel, n, tm), [shape((n * tm, 8, LANES),...]
    pallas_call x1 -> x0, Pallas kernels: 0.89 us -> none  [shards(): call(functools.partial(coef_kernel, n), [shape((384, 2 * LANES), bf16)] *...]
  transfers between devices with their start and end apart: 1 -> 0, of which waited for: 1 -> 0; matrix products, arithmetic and copies ran while one was open for 0% -> 0% of each run, Pallas kernels for 2% -> 0%
where the time goes in v4:
time: 35.9 us; the launch traced here: 35.7 us
  blocking collectives  31.4 us (87%)
  Pallas kernels  3.64 us (10%)
  between operations  0.66 us (2%)
    all_to_all x1, blocking collectives, shards(): lax.all_to_all(outgoing, 'tile', split_axis=0, concat_axis=0, tiled=True)  19.5 us
    all_to_all x1, blocking collectives, shards(): lax.all_to_all(message, ('tile', 'tm'), split_axis=0, concat_axis=0, tile...  11.9 us
    pallas_call x1, Pallas kernels, shards(): call(functools.partial(pack_kernel, n), [shape((n, DATA_ROWS + META_ROWS,...  1.36 us
    pallas_call x1, Pallas kernels, shards(): call(functools.partial(sweep_kernel, n, tm), [shape((8, LANES), f32), sha...  1.28 us
    pallas_call x1, Pallas kernels, shards(): call(functools.partial(project_kernel, n, tm), [shape((n * tm, 8, LANES),...  1 us

profile of v4, /device:TPU:0, one launch (start us, length us, event | category | flops | bytes accessed | tf_op | source)
XLA Modules:
  0.0 35.7 jit_solution(4090645518151969182)
XLA Ops:
  0.6 1.4 %shard_map.95 = (bf16[16,96,128]{2,1,0:T(8,128)(2,1)S(1)}, f32[40,128]{1,0:T(8,128)S(1)}) custom-call(s32[8,16]{1,0:T(8,128)} %bitcast.10, bf16[128,8,128]{2,1,0:T(8,128)(2,1)} %refs_1_.1, s32[1,128]{1,0:T(1,128)} %bitcast.14, s32[8,128]{1,0:T(8,128)} %bitcast.11, f32[8,128]{1,0:T(8,128)} %bitcast.12, f32[8,128]{1,0:T(8,128)} %refs_5_.1, s32[8,128]{1,0:T(8,128)} %bitcast.13), custom_call_target="tpu_custom_call" | custom-call | tf_op jit(solution)/shard_map/pallas_call | solution.py:313
  2.0 0.0 copy-start
  2.0 19.5 %all_to_all.10.recv_ref = bf16[16,96,128]{2,1,0:T(8,128)(2,1)S(1)} all-to-all(bf16[16,96,128]{2,1,0:T(8,128)(2,1)S(1)} %get-tuple-element.10), channel_id=1, replica_groups=mesh['tile'=16,'tm'=2] {'tile'}, dimensions={0} | all-to-all | bytes 786432 | tf_op jit(solution)/shard_map/all_to_all | solution.py:322
  21.5 0.0 copy-done
  21.5 1.0 %shard_map.96 = (f32[32,8,128]{2,1,0:T(8,128)S(1)}, f32[8,128]{1,0:T(8,128)S(1)}, s32[32,128]{1,0:T(8,128)S(1)}, f32[96,128]{1,0:T(8,128)S(1)}) custom-call(bf16[16,96,128]{2,1,0:T(8,128)(2,1)S(1)} %all_to_all.10.recv_ref, bf16[1024,128]{1,0:T(8,128)(2,1)S(1)} %bitcast.9, f32[40,128]{1,0:T(8,128)S(1)} %get-tuple-element.11.own_ref), custom_call_target="tpu_custom_call" | custom-call | tf_op jit(solution)/shard_map/pallas_call | solution.py:324
  22.5 11.9 %all_to_all.11.recv_ref = f32[32,8,128]{2,1,0:T(8,128)S(1)} all-to-all(f32[32,8,128]{2,1,0:T(8,128)S(1)} %get-tuple-element.12), channel_id=1, replica_groups=mesh['tile'=16,'tm'=2] {'tile','tm'}, dimensions={0} | all-to-all | bytes 262144 | tf_op jit(solution)/shard_map/all_to_all | solution.py:331
  34.4 1.3 %shard_map.97 = (f32[8,128]{1,0:T(8,128)}, f32[1,128]{1,0:T(1,128)}) custom-call(f32[32,8,128]{2,1,0:T(8,128)S(1)} %all_to_all.11.recv_ref, f32[8,128]{1,0:T(8,128)S(1)} %get-tuple-element.13.gram_ref, f32[40,128]{1,0:T(8,128)S(1)} %get-tuple-element.11.own_ref, s32[32,128]{1,0:T(8,128)S(1)} %get-tuple-element.14.lanes_ref, ...), custom_call_target="tpu_custom_call" | custom-call | tf_op jit(solution)/shard_map/pallas_call | solution.py:332
Async XLA Ops:
  2.0 19.5 %copy-start = (bf16[128,8,128]{2,1,0:T(8,128)(2,1)S(1)}, bf16[128,8,128]{2,1,0:T(8,128)(2,1)}, u32[]{:S(2)}) copy-start(bf16[128,8,128]{2,1,0:T(8,128)(2,1)} %param.11) | copy-start | bytes 786436

commit v5 on v4

--- a/solution.py
+++ b/solution.py
@@ -16,7 +16,8 @@
 LANES = 128
 QUARTER = 32
 DATA_ROWS = 64
-META_ROWS = 32
+META_ROWS = 24
+LOW_SENT = 6
 GROUP = 4
 VMEM_LIMIT = 48 * 2 ** 20
 PACK_LIMIT = 48 * 2 ** 20
@@ -64,14 +65,14 @@
 
 def pack_kernel(n, *refs):
     sources, (out_ref, own_ref), held, sems = refs[:7], refs[7:9], refs[9:16], refs[16]
-    send_ref, data_ref, colour_ref, corr_ref, gram_ref, init_ref, slot_ref = held
+    colour_ref, corr_ref, gram_ref, init_ref, slot_ref, send_ref, data_ref = held
     copies = [pltpu.make_async_copy(a, b, sems.at[i]) for i, (a, b) in enumerate(zip(sources, held))]
     for copy in copies:
         copy.start()
     me = lax.axis_index("tile")
     lane = iota((8, LANES), 1)
     row = iota((8, LANES), 0)
-    for copy in copies[2:]:
+    for copy in copies[:5]:
         copy.wait()
     own_ref[24:32, :] = slot_ref[...].astype(jnp.float32)
     pos = places(colour_ref[...])
@@ -84,22 +85,30 @@
     gram = gram_ref[...]
     gram_hi, gram_lo = split2(gram)
     init_hi, init_lo = split2(init_ref[...])
-    rows = [code, gram_hi, gram_lo, lane.astype(jnp.float32)]
+    rows = [code, gram_hi, gram_lo, init_hi, init_lo, lane.astype(jnp.float32)]
     placed = dot_nt(jnp.concatenate(rows, axis=0).astype(jnp.bfloat16), order)
+    placed = [placed[8 * i : 8 * i + 8] for i in range(6)]
+    pos = jnp.broadcast_to(pos, (8, LANES))
     own_ref[0:8, :] = code
     own_ref[8:16, :] = gram
-    own_ref[16:24, :] = jnp.broadcast_to(pos, (8, LANES))
-    own_ref[32:40, :] = placed[24:32]
-    first = jnp.where(lane < 64, pltpu.roll(placed[0:8], 96, 1), pltpu.roll(placed[8:16], 32, 1))
-    spread = jnp.where(row == 0, pltpu.roll(jnp.broadcast_to(pos, (8, LANES)), 64, 1), pos)
-    second = jnp.where(lane < 64, pltpu.roll(placed[16:24], 96, 1), spread)
-    meta = jnp.concatenate([first, second, init_hi, init_lo], axis=0).astype(jnp.bfloat16)
-    for copy in copies[:2]:
+    own_ref[16:24, :] = pos
+    own_ref[32:40, :] = placed[5]
+    first = jnp.where(lane < 64, pltpu.roll(placed[0], 96, 1), pltpu.roll(placed[1], 32, 1))
+    tails = []
+    for low, even, odd in ((64, 96, 64), (32, 32, 0)):
+        even = pltpu.roll(pos, even, 1)
+        odd = pltpu.roll(pos, odd, 1) if odd else pos
+        tails.append(
+            jnp.where(row < LOW_SENT, pltpu.roll(placed[2], low, 1), jnp.where(row == LOW_SENT, even, odd))
+        )
+    second = jnp.where(lane < 96, pltpu.roll(placed[3], 96, 1), tails[0])
+    third = jnp.where(lane < 96, pltpu.roll(placed[4], 96, 1), tails[1])
+    meta = jnp.concatenate([first, second, third], axis=0)
+    for copy in copies[5:]:
         copy.wait()
     for target in range(n):
-        out_ref[target, DATA_ROWS:, :] = meta
         blocks = [data_ref[send_ref[c, target]].astype(jnp.float32) for c in range(8)]
-        out_ref[target, :DATA_ROWS, :] = jnp.concatenate(blocks, axis=0).astype(jnp.bfloat16)
+        out_ref[target] = jnp.concatenate(blocks + [meta], axis=0).astype(jnp.bfloat16)
 
 
 def lookup(table, index):
@@ -163,21 +172,24 @@
     projected = total[:, :LANES]
     for j in range(1, 8):
         projected = projected + total[:, j * LANES : (j + 1) * LANES]
-    metas = [recv_ref[tile_at(me, rel, n), DATA_ROWS:, :].astype(jnp.float32) for rel in REACH]
+    block = lax.shift_right_logical(lane, 5)
+    metas = [recv_ref[tile_at(me, rel, n)].astype(jnp.float32)[DATA_ROWS:] for rel in REACH]
     places_of = []
     for meta in metas:
-        found = jnp.where(lane < 64, pltpu.roll(spread_row(meta, 8), 64, 1), spread_row(meta, 9))
-        places_of.append(found)
+        parts = [spread_row(meta, 8 + LOW_SENT), spread_row(meta, 9 + LOW_SENT)]
+        parts += [spread_row(meta, 16 + LOW_SENT), spread_row(meta, 17 + LOW_SENT)]
+        parts = [pltpu.roll(part, 32 * i + 32, 1) if i < 3 else part for i, part in enumerate(parts)]
+        places_of.append(pick(parts, block))
     code = own_ref[0:8, :].astype(jnp.int32) + 2 * LANES
     index, which = jnp.bitwise_and(code, LANES - 1), lax.shift_right_logical(code, 7)
     place = pick([lookup(places_of[r], index) for r in range(4)], which).astype(jnp.int32)
     own_place = own_ref[16:24, :].astype(jnp.int32)
     after = lax.shift_right_logical(place, 5) > lax.shift_right_logical(own_place, 5)
     late = jnp.where(after, own_ref[8:16, :], 0.0)
-    starts = [meta[16:24] + meta[24:32] for meta in metas[:4]]
+    starts = [pltpu.roll(meta[8:16] + meta[16:24], 32, 1) for meta in metas[:4]]
     held = None
     for i in range(8):
-        at, owner = spread_row(index, i), spread_row(which, i)
+        at, owner = spread_row(place, i), spread_row(which, i)
         term = pick([lookup(start, at) for start in starts], owner) * spread_row(late, i)
         held = term if held is None else held + term
     names = own_ref[32:40, :].astype(jnp.int32)
@@ -185,8 +197,12 @@
     gram = lookup(gram, names)
     gram_ref[...] = gram
     message = jnp.where(lane < QUARTER, jnp.maximum(base / gram, 0.0), base)
-    grams12 = jnp.where(row == 0, pltpu.roll(gram, 64, 1), pltpu.roll(gram, 32, 1))
-    others = jnp.where(lane < 96, message, grams12)
+    listed = lookup(own_ref[8:16, :], names)
+    rest = split2(listed)[1]
+    spare = jnp.where(row < 4, spread_row(rest, LOW_SENT), spread_row(rest, LOW_SENT + 1))
+    spare = jnp.where(row < 2, gram, spare)
+    spare = jnp.where(jnp.bitwise_and(row, 1) == 0, pltpu.roll(spare, 64, 1), pltpu.roll(spare, 32, 1))
+    others = jnp.where(lane < 96, message, spare)
     for t in range(n * tm):
         out_ref[t] = others
     for i, rel in enumerate(REACH):
@@ -195,7 +211,6 @@
         target = tile_at(me, (-rel[0], rel[1]), n)
         for t in range(tm):
             out_ref[target * tm + t] = turned
-    block = lax.shift_right_logical(lane, 5)
     codes = []
     for i in range(8):
         code = metas[i][0:8].astype(jnp.int32) + 2 * LANES
@@ -213,17 +228,20 @@
             out = turned if out is None else jnp.where(block == p, turned, out)
         return out
 
-    hi, low = [meta[0:8] for meta in metas[:8]], [meta[8:16] for meta in metas[:8]]
+    high = [meta[0:8] for meta in metas[:8]]
     slot = 0
     for step, (group, colour) in enumerate(((0, 1), (1, 1), (0, 2), (0, 3))):
         if step < 3:
             start = QUARTER * (colour - 1)
             code = gathered(codes, group, colour, start).astype(jnp.int32)
-            weight = gathered(hi, group, colour, start + 64) + gathered(low, group, colour, start)
+            low = [jnp.where(row < LOW_SENT, meta[8 * colour : 8 * colour + 8], 0.0) for meta in metas[:8]]
+            weight = gathered(high, group, colour, start + 64) + gathered(low, group, colour, 96)
+            if group == 0:
+                weight = jnp.where(block == colour, listed, weight)
             device, at = lax.shift_right_logical(code, 7), jnp.bitwise_and(code, LANES - 1)
             devices = range(12) if step == 1 else range(8)
         else:
-            weight = lookup(own_ref[8:16, :], names)
+            weight = listed
             device, at = lookup(which, names), lookup(index, names)
             devices = range(4)
         lanes, parts = edges(devices, places_of, device, at, weight, SOURCES[step])
@@ -248,19 +266,26 @@
                 out = jnp.where(block == (q + turn) % 4, messages[4 * group + q], out)
         return out
 
-    def gram_of(messages, group, colour):
-        rows = spread_row(gathered(messages, group, 3), colour - 1)
-        rows = pltpu.roll(rows, 64 if colour == 1 else 96, 1)
+    def spare_of(messages, group, colour):
+        return pltpu.roll(gathered(messages, group, 3), 64 if colour == 1 else 96, 1)
+
+    def gram_of(spare, group, colour):
+        rows = spread_row(spare, colour - 1)
         return jnp.where(block == colour, gram, rows) if group == 0 else rows
 
-    def neighbours(step, tiles):
+    def neighbours(step, tiles, spare, group, colour):
         slot = sum(len(sources) for sources in SOURCES[:step])
         total = None
         for i in range(8):
             at = jnp.broadcast_to(lanes_ref[8 * step + i : 8 * step + i + 1, :], (8, LANES))
             for s, tile in enumerate(tiles):
                 place = 8 * (slot + s) + i
-                term = lookup(tile, at) * weights_ref[place : place + 1, :]
+                weight = jnp.broadcast_to(weights_ref[place : place + 1, :], (8, LANES))
+                if spare is not None and i >= LOW_SENT:
+                    low = spread_row(spare, 2 * (i - LOW_SENT) + 1 + colour)
+                    low = jnp.where(block == colour, 0.0, low) if group == 0 else low
+                    weight = jnp.where(weight != 0.0, weight + low, 0.0)
+                term = lookup(tile, at) * weight
                 total = term if total is None else total + term
         return total
 
@@ -270,11 +295,13 @@
         x0 = [gathered(messages, group, 0) for group in range(3)]
         x1 = []
         for group in range(2):
-            fresh = gathered(messages, group, 1) - neighbours(group, x0[: 2 + group])
-            x1.append(jnp.maximum(fresh / gram_of(messages, group, 1), 0.0))
-        fresh = gathered(messages, 0, 2) - neighbours(2, [x0[0], x0[1], x1[0], x1[1]])
-        x2 = jnp.maximum(fresh / gram_of(messages, 0, 2), 0.0)
-        fresh = messages[0] - neighbours(3, [x0[0], x1[0], x2])
+            spare = spare_of(messages, group, 1)
+            fresh = gathered(messages, group, 1) - neighbours(group, x0[: 2 + group], spare, group, 1)
+            x1.append(jnp.maximum(fresh / gram_of(spare, group, 1), 0.0))
+        spare = spare_of(messages, 0, 2)
+        fresh = gathered(messages, 0, 2) - neighbours(2, [x0[0], x0[1], x1[0], x1[1]], spare, 0, 2)
+        x2 = jnp.maximum(fresh / gram_of(spare, 0, 2), 0.0)
+        fresh = messages[0] - neighbours(3, [x0[0], x1[0], x2], None, 0, 3)
         x3 = jnp.maximum(fresh / gram, 0.0)
         own = pick([messages[0], x1[0], x2, x3], block)
         square = jnp.sum(own * own, axis=0, keepdims=True)
@@ -307,15 +334,15 @@
         )
 
     inputs = (
-        send_list[0].T, data, colour.reshape(1, LANES), correlation.T, correlation_gram.T, traces_init,
-        footprint_slot.T,
+        colour.reshape(1, LANES), correlation.T, correlation_gram.T, traces_init, footprint_slot.T,
+        send_list[0].T, data,
     )
     outgoing, own = call(
         functools.partial(pack_kernel, n),
         [shape((n, DATA_ROWS + META_ROWS, LANES), bf16), shape((40, LANES), f32)],
         [hbm] * 7,
-        [pltpu.SMEM(inputs[0].shape, jnp.int32)]
-        + [pltpu.VMEM(x.shape, x.dtype) for x in inputs[1:]]
+        [pltpu.VMEM(x.shape, x.dtype) for x in inputs[:5]]
+        + [pltpu.SMEM(inputs[5].shape, jnp.int32), pltpu.VMEM(data.shape, bf16)]
         + [pltpu.SemaphoreType.DMA((7,))],
         PACK_LIMIT,
     )(*[pltpu.with_memory_space_constraint(x, pltpu.HBM) for x in inputs])

time: 35.9 us -> 35.1 us (0.978)
  blocking collectives: 31.4 us -> 30.7 us
    all_to_all x1, blocking collectives: 19.5 us -> 19 us  [shards(): lax.all_to_all(outgoing, 'tile', split_axis=0, concat_axis=0, tiled=True)]
where the time goes in v5:
time: 35.1 us; the launch traced here: 34.9 us
  blocking collectives  30.7 us (87%)
  Pallas kernels  3.6 us (10%)
  between operations  0.65 us (2%)
    all_to_all x1, blocking collectives, shards(): lax.all_to_all(outgoing, 'tile', split_axis=0, concat_axis=0, tiled=True)  19 us
    all_to_all x1, blocking collectives, shards(): lax.all_to_all(message, ('tile', 'tm'), split_axis=0, concat_axis=0, tile...  11.7 us
    pallas_call x1, Pallas kernels, shards(): call(functools.partial(sweep_kernel, n, tm), [shape((8, LANES), f32), sha...  1.31 us
    pallas_call x1, Pallas kernels, shards(): call(functools.partial(pack_kernel, n), [shape((n, DATA_ROWS + META_ROWS,...  1.29 us
    pallas_call x1, Pallas kernels, shards(): call(functools.partial(project_kernel, n, tm), [shape((n * tm, 8, LANES),...  1 us

profile of v5, /device:TPU:0, one launch (start us, length us, event | category | flops | bytes accessed | tf_op | source)
XLA Modules:
  0.0 34.9 jit_solution(7185621798634234934)
XLA Ops:
  0.6 1.3 %shard_map.95 = (bf16[16,88,128]{2,1,0:T(8,128)(2,1)S(1)}, f32[40,128]{1,0:T(8,128)S(1)}) custom-call(s32[1,128]{1,0:T(1,128)} %bitcast.14, s32[8,128]{1,0:T(8,128)} %bitcast.10, f32[8,128]{1,0:T(8,128)} %bitcast.11, f32[8,128]{1,0:T(8,128)} %refs_3_.1, s32[8,128]{1,0:T(8,128)} %bitcast.12, s32[8,16]{1,0:T(8,128)} %bitcast.13, bf16[128,8,128]{2,1,0:T(8,128)(2,1)} %refs_6_.1), custom_call_target="tpu_custom_call" | custom-call | tf_op jit(solution)/shard_map/pallas_call | solution.py:340
  1.9 0.0 copy-start
  1.9 19.0 %all_to_all.10.recv_ref = bf16[16,88,128]{2,1,0:T(8,128)(2,1)S(1)} all-to-all(bf16[16,88,128]{2,1,0:T(8,128)(2,1)S(1)} %get-tuple-element.10), channel_id=1, replica_groups=mesh['tile'=16,'tm'=2] {'tile'}, dimensions={0} | all-to-all | bytes 720896 | tf_op jit(solution)/shard_map/all_to_all | solution.py:349
  20.9 0.0 copy-done
  20.9 1.0 %shard_map.96 = (f32[32,8,128]{2,1,0:T(8,128)S(1)}, f32[8,128]{1,0:T(8,128)S(1)}, s32[32,128]{1,0:T(8,128)S(1)}, f32[96,128]{1,0:T(8,128)S(1)}) custom-call(bf16[16,88,128]{2,1,0:T(8,128)(2,1)S(1)} %all_to_all.10.recv_ref, bf16[1024,128]{1,0:T(8,128)(2,1)S(1)} %bitcast.9, f32[40,128]{1,0:T(8,128)S(1)} %get-tuple-element.11.own_ref), custom_call_target="tpu_custom_call" | custom-call | tf_op jit(solution)/shard_map/pallas_call | solution.py:351
  21.9 11.7 %all_to_all.11.recv_ref = f32[32,8,128]{2,1,0:T(8,128)S(1)} all-to-all(f32[32,8,128]{2,1,0:T(8,128)S(1)} %get-tuple-element.12), channel_id=1, replica_groups=mesh['tile'=16,'tm'=2] {'tile','tm'}, dimensions={0} | all-to-all | bytes 262144 | tf_op jit(solution)/shard_map/all_to_all | solution.py:358
  33.6 1.3 %shard_map.97 = (f32[8,128]{1,0:T(8,128)}, f32[1,128]{1,0:T(1,128)}) custom-call(f32[32,8,128]{2,1,0:T(8,128)S(1)} %all_to_all.11.recv_ref, f32[8,128]{1,0:T(8,128)S(1)} %get-tuple-element.13.gram_ref, f32[40,128]{1,0:T(8,128)S(1)} %get-tuple-element.11.own_ref, s32[32,128]{1,0:T(8,128)S(1)} %get-tuple-element.14.lanes_ref, ...), custom_call_target="tpu_custom_call" | custom-call | tf_op jit(solution)/shard_map/pallas_call | solution.py:359
Async XLA Ops:
  1.9 19.0 %copy-start = (bf16[128,8,128]{2,1,0:T(8,128)(2,1)S(1)}, bf16[128,8,128]{2,1,0:T(8,128)(2,1)}, u32[]{:S(2)}) copy-start(bf16[128,8,128]{2,1,0:T(8,128)(2,1)} %param.11) | copy-start | bytes 786436

commit v6 on v5

--- a/solution.py
+++ b/solution.py
@@ -13,6 +13,13 @@
     (3, 0), (-3, 0), (2, 1), (-2, 1),
 )
 NEAR = REACH[:4]
+ORDERS = {
+    (16, 2): (
+        [5, 0, 9, 8, 14, 2, 4, 12, 3, 1, 11, 10, 6, 7, 13, 15],
+        [0, 17, 26, 21, 1, 25, 7, 24, 29, 9, 16, 5, 22, 12, 18, 8]
+        + [13, 20, 28, 14, 19, 3, 2, 4, 23, 31, 27, 10, 6, 11, 15, 30],
+    ),
+}
 LANES = 128
 QUARTER = 32
 DATA_ROWS = 64
@@ -36,6 +43,20 @@
     return lax.rem(me + rel[0] + rel[1] * (n // 2) + n, n)
 
 
+def slots_of(order):
+    return [order.index(device) for device in range(len(order))]
+
+
+def entry(table, i):
+    if table == list(range(len(table))):
+        return i
+    words = [sum(table[w + b] << (8 * b) for b in range(4)) for w in range(0, len(table), 4)]
+    word, at = words[0], lax.shift_right_logical(i, 2)
+    for w in range(1, len(words)):
+        word = jnp.where(at == w, words[w], word)
+    return jnp.bitwise_and(lax.shift_right_logical(word, 8 * jnp.bitwise_and(i, 3)), 255)
+
+
 def dot(a, b):
     return jnp.dot(a, b, preferred_element_type=jnp.float32)
 
@@ -63,7 +84,7 @@
     return rank + (colour_row * QUARTER).astype(jnp.float32)
 
 
-def pack_kernel(n, *refs):
+def pack_kernel(n, slots, *refs):
     sources, (out_ref, own_ref), held, sems = refs[:7], refs[7:9], refs[9:16], refs[16]
     colour_ref, corr_ref, gram_ref, init_ref, slot_ref, send_ref, data_ref = held
     copies = [pltpu.make_async_copy(a, b, sems.at[i]) for i, (a, b) in enumerate(zip(sources, held))]
@@ -108,7 +129,7 @@
         copy.wait()
     for target in range(n):
         blocks = [data_ref[send_ref[c, target]].astype(jnp.float32) for c in range(8)]
-        out_ref[target] = jnp.concatenate(blocks + [meta], axis=0).astype(jnp.bfloat16)
+        out_ref[slots[target]] = jnp.concatenate(blocks + [meta], axis=0).astype(jnp.bfloat16)
 
 
 def lookup(table, index):
@@ -147,7 +168,7 @@
 )
 
 
-def project_kernel(n, tm, recv_ref, fp_ref, own_ref, out_ref, gram_ref, lanes_ref, weights_ref, wide_ref):
+def project_kernel(n, tm, slots, message_slots, recv_ref, fp_ref, own_ref, out_ref, gram_ref, lanes_ref, weights_ref, wide_ref):
     me = lax.axis_index("tile")
     lane = iota((8, LANES), 1)
     row = iota((8, LANES), 0)
@@ -164,7 +185,8 @@
     slot_row = jnp.broadcast_to(slot_row, (8, 8 * LANES))
     total = jnp.zeros((8, 8 * LANES), jnp.float32)
     for source in range(0, n, GROUP):
-        blocks = recv_ref[source : source + GROUP, :DATA_ROWS, :].reshape(GROUP * DATA_ROWS, LANES)
+        blocks = [recv_ref[slots[source + i], :DATA_ROWS, :] for i in range(GROUP)]
+        blocks = jnp.concatenate(blocks, axis=0)
         product = dot_nt(blocks, weights)
         for c in range(GROUP * 8):
             hit = slot_row == float(source * 8 + c)
@@ -173,7 +195,7 @@
     for j in range(1, 8):
         projected = projected + total[:, j * LANES : (j + 1) * LANES]
     block = lax.shift_right_logical(lane, 5)
-    metas = [recv_ref[tile_at(me, rel, n)].astype(jnp.float32)[DATA_ROWS:] for rel in REACH]
+    metas = [recv_ref[entry(slots, tile_at(me, rel, n))].astype(jnp.float32)[DATA_ROWS:] for rel in REACH]
     places_of = []
     for meta in metas:
         parts = [spread_row(meta, 8 + LOW_SENT), spread_row(meta, 9 + LOW_SENT)]
@@ -210,7 +232,7 @@
         turned = source if i % 4 == 0 else pltpu.roll(source, QUARTER * (i % 4), 1)
         target = tile_at(me, (-rel[0], rel[1]), n)
         for t in range(tm):
-            out_ref[target * tm + t] = turned
+            out_ref[entry(message_slots, target * tm + t)] = turned
     codes = []
     for i in range(8):
         code = metas[i][0:8].astype(jnp.int32) + 2 * LANES
@@ -251,7 +273,7 @@
             slot += 1
 
 
-def sweep_kernel(n, tm, recv_ref, gram_ref, own_ref, lanes_ref, weights_ref, traces_ref, rms_ref):
+def sweep_kernel(n, tm, message_slots, recv_ref, gram_ref, own_ref, lanes_ref, weights_ref, traces_ref, rms_ref):
     me = lax.axis_index("tile")
     half = lax.axis_index("tm")
     lane = iota((8, LANES), 1)
@@ -291,7 +313,7 @@
 
     energy, mine = None, None
     for t in range(tm):
-        messages = [recv_ref[f + t] for f in first]
+        messages = [recv_ref[entry(message_slots, f + t)] for f in first]
         x0 = [gathered(messages, group, 0) for group in range(3)]
         x1 = []
         for group in range(2):
@@ -318,6 +340,7 @@
 ):
     n = lax.axis_size("tile")
     tm = lax.axis_size("tm")
+    tiles, devices = ORDERS.get((n, tm), (list(range(n)), list(range(n * tm))))
     f32, bf16 = jnp.float32, jnp.bfloat16
     shape = jax.ShapeDtypeStruct
     vmem = pl.BlockSpec(memory_space=pltpu.VMEM)
@@ -338,7 +361,7 @@
         send_list[0].T, data,
     )
     outgoing, own = call(
-        functools.partial(pack_kernel, n),
+        functools.partial(pack_kernel, n, slots_of(tiles)),
         [shape((n, DATA_ROWS + META_ROWS, LANES), bf16), shape((40, LANES), f32)],
         [hbm] * 7,
         [pltpu.VMEM(x.shape, x.dtype) for x in inputs[:5]]
@@ -346,18 +369,22 @@
         + [pltpu.SemaphoreType.DMA((7,))],
         PACK_LIMIT,
     )(*[pltpu.with_memory_space_constraint(x, pltpu.HBM) for x in inputs])
-    arrived = lax.all_to_all(outgoing, "tile", split_axis=0, concat_axis=0, tiled=True)
+    arrived = lax.all_to_all(
+        outgoing, "tile", split_axis=0, concat_axis=0, tiled=True, axis_index_groups=[tiles]
+    )
     slots = sum(len(sources) for sources in SOURCES)
     message, gram, lanes, weights = call(
-        functools.partial(project_kernel, n, tm),
+        functools.partial(project_kernel, n, tm, slots_of(tiles), slots_of(devices)),
         [shape((n * tm, 8, LANES), f32), shape((8, LANES), f32)]
         + [shape((8 * len(SOURCES), LANES), jnp.int32), shape((8 * slots, LANES), f32)],
         [vmem] * 3,
         [pltpu.VMEM((8 * LANES, LANES), f32)],
     )(arrived, footprint.reshape(8 * LANES, LANES), own)
-    messages = lax.all_to_all(message, ("tile", "tm"), split_axis=0, concat_axis=0, tiled=True)
+    messages = lax.all_to_all(
+        message, ("tile", "tm"), split_axis=0, concat_axis=0, tiled=True, axis_index_groups=[devices]
+    )
     traces, rms = call(
-        functools.partial(sweep_kernel, n, tm),
+        functools.partial(sweep_kernel, n, tm, slots_of(devices)),
         [shape((8, LANES), f32), shape((1, LANES), f32)],
         [vmem] * 5,
     )(messages, gram, own, lanes, weights)

time: 35.1 us -> 32.6 us (0.929)
  blocking collectives: 30.7 us -> 28.1 us
    all_to_all x1, blocking collectives: 19 us -> 17.3 us  [shards(): lax.all_to_all(outgoing, 'tile', split_axis=0, concat_axis=0, tiled=True,...]
    all_to_all x1, blocking collectives: 11.7 us -> 10.8 us  [shards(): lax.all_to_all(message, ('tile', 'tm'), split_axis=0, concat_axis=0, tile...]
where the time goes in v6:
time: 32.6 us; the launch traced here: 32.4 us
  blocking collectives  28.1 us (86%)
  Pallas kernels  3.64 us (11%)
  between operations  0.66 us (2%)
    all_to_all x1, blocking collectives, shards(): lax.all_to_all(outgoing, 'tile', split_axis=0, concat_axis=0, tiled=True,...  17.3 us
    all_to_all x1, blocking collectives, shards(): lax.all_to_all(message, ('tile', 'tm'), split_axis=0, concat_axis=0, tile...  10.8 us
    pallas_call x1, Pallas kernels, shards(): call(functools.partial(sweep_kernel, n, tm, slots_of(devices)), [shape((8...  1.34 us
    pallas_call x1, Pallas kernels, shards(): call(functools.partial(pack_kernel, n, slots_of(tiles)), [shape((n, DATA_...  1.29 us
    pallas_call x1, Pallas kernels, shards(): call(functools.partial(project_kernel, n, tm, slots_of(tiles), slots_of(d...  1.01 us

profile of v6, /device:TPU:0, one launch (start us, length us, event | category | flops | bytes accessed | tf_op | source)
XLA Modules:
  0.0 32.4 jit_solution(7324216505440573172)
XLA Ops:
  0.6 1.3 %shard_map.95 = (bf16[16,88,128]{2,1,0:T(8,128)(2,1)S(1)}, f32[40,128]{1,0:T(8,128)S(1)}) custom-call(s32[1,128]{1,0:T(1,128)} %bitcast.14, s32[8,128]{1,0:T(8,128)} %bitcast.10, f32[8,128]{1,0:T(8,128)} %bitcast.11, f32[8,128]{1,0:T(8,128)} %refs_3_.1, s32[8,128]{1,0:T(8,128)} %bitcast.12, s32[8,16]{1,0:T(8,128)} %bitcast.13, bf16[128,8,128]{2,1,0:T(8,128)(2,1)} %refs_6_.1), custom_call_target="tpu_custom_call" | custom-call | tf_op jit(solution)/shard_map/pallas_call | solution.py:363
  1.9 0.0 copy-start
  1.9 17.3 %all_to_all.10.recv_ref = bf16[16,88,128]{2,1,0:T(8,128)(2,1)S(1)} all-to-all(bf16[16,88,128]{2,1,0:T(8,128)(2,1)S(1)} %get-tuple-element.10), channel_id=1, replica_groups={{10,0,18,16,28,4,8,24,6,2,22,20,12,14,26,30},{11,1,19,17,29,5,9,25,7,3,..., dimensions={0} | all-to-all | bytes 720896 | tf_op jit(solution)/shard_map/all_to_all | solution.py:372
  19.2 0.0 copy-done
  19.2 1.0 %shard_map.96 = (f32[32,8,128]{2,1,0:T(8,128)S(1)}, f32[8,128]{1,0:T(8,128)S(1)}, s32[32,128]{1,0:T(8,128)S(1)}, f32[96,128]{1,0:T(8,128)S(1)}) custom-call(bf16[16,88,128]{2,1,0:T(8,128)(2,1)S(1)} %all_to_all.10.recv_ref, bf16[1024,128]{1,0:T(8,128)(2,1)S(1)} %bitcast.9, f32[40,128]{1,0:T(8,128)S(1)} %get-tuple-element.11.own_ref), custom_call_target="tpu_custom_call" | custom-call | tf_op jit(solution)/shard_map/pallas_call | solution.py:376
  20.2 10.8 %all_to_all.11.recv_ref = f32[32,8,128]{2,1,0:T(8,128)S(1)} all-to-all(f32[32,8,128]{2,1,0:T(8,128)S(1)} %get-tuple-element.12), channel_id=1, replica_groups={{0,17,26,21,1,25,7,24,29,9,16,5,22,12,18,8,13,20,28,14,19,3,2,4,23,31,2..., dimensions={0} | all-to-all | bytes 262144 | tf_op jit(solution)/shard_map/all_to_all | solution.py:383
  31.0 1.3 %shard_map.97 = (f32[8,128]{1,0:T(8,128)}, f32[1,128]{1,0:T(1,128)}) custom-call(f32[32,8,128]{2,1,0:T(8,128)S(1)} %all_to_all.11.recv_ref, f32[8,128]{1,0:T(8,128)S(1)} %get-tuple-element.13.gram_ref, f32[40,128]{1,0:T(8,128)S(1)} %get-tuple-element.11.own_ref, s32[32,128]{1,0:T(8,128)S(1)} %get-tuple-element.14.lanes_ref, ...), custom_call_target="tpu_custom_call" | custom-call | tf_op jit(solution)/shard_map/pallas_call | solution.py:386
Async XLA Ops:
  1.9 17.3 %copy-start = (bf16[128,8,128]{2,1,0:T(8,128)(2,1)S(1)}, bf16[128,8,128]{2,1,0:T(8,128)(2,1)}, u32[]{:S(2)}) copy-start(bf16[128,8,128]{2,1,0:T(8,128)(2,1)} %param.11) | copy-start | bytes 786436

commit v7 on v6

--- a/solution.py
+++ b/solution.py
@@ -15,7 +15,7 @@
 NEAR = REACH[:4]
 ORDERS = {
     (16, 2): (
-        [5, 0, 9, 8, 14, 2, 4, 12, 3, 1, 11, 10, 6, 7, 13, 15],
+        [5, 1, 4, 10, 9, 15, 14, 12, 3, 2, 11, 8, 6, 7, 13, 0],
         [0, 17, 26, 21, 1, 25, 7, 24, 29, 9, 16, 5, 22, 12, 18, 8]
         + [13, 20, 28, 14, 19, 3, 2, 4, 23, 31, 27, 10, 6, 11, 15, 30],
     ),
@@ -132,8 +132,13 @@
         out_ref[slots[target]] = jnp.concatenate(blocks + [meta], axis=0).astype(jnp.bfloat16)
 
 
+def column(row):
+    eye = iota((LANES, LANES), 0) == iota((LANES, LANES), 1)
+    return dot(jnp.where(eye, row, 0.0).astype(jnp.bfloat16), jnp.ones((LANES, LANES), jnp.bfloat16))
+
+
 def lookup(table, index):
-    return jnp.take_along_axis(table, index, axis=1)
+    return jnp.take_along_axis(table, index, axis=1, mode="promise_in_bounds")
 
 
 def spread_row(rows, i):
@@ -174,20 +179,26 @@
     row = iota((8, LANES), 0)
     wide_ref[...] = fp_ref[...].astype(jnp.float32)
     weights, squares = [], None
+    cut = 4 * n
+    upper = (own_ref[24:32, :] >= float(cut)).astype(jnp.float32)
     for j in range(8):
         rows = wide_ref[pl.ds(j, LANES, stride=8), :]
-        weights.append(rows.astype(jnp.bfloat16))
         squares = rows * rows if j == 0 else squares + rows * rows
+        above = column(upper[j : j + 1]) * rows
+        weights.append(jnp.concatenate([rows - above, above], axis=1).astype(jnp.bfloat16))
     weights = jnp.concatenate(weights, axis=0)
     gram = dot_nt(jnp.ones((8, LANES), jnp.bfloat16), split3(squares))
     gram = gram[:, :LANES] + gram[:, LANES : 2 * LANES] + gram[:, 2 * LANES :]
-    slot_row = jnp.concatenate([own_ref[24 + j : 25 + j, :] for j in range(8)], axis=1)
+    slot_rows = own_ref[24:32, :] - upper * float(cut)
+    slot_row = jnp.concatenate([slot_rows[j : j + 1] for j in range(8)], axis=1)
     slot_row = jnp.broadcast_to(slot_row, (8, 8 * LANES))
     total = jnp.zeros((8, 8 * LANES), jnp.float32)
-    for source in range(0, n, GROUP):
-        blocks = [recv_ref[slots[source + i], :DATA_ROWS, :] for i in range(GROUP)]
-        blocks = jnp.concatenate(blocks, axis=0)
-        product = dot_nt(blocks, weights)
+    for source in range(0, n // 2, GROUP):
+        halves = []
+        for first in (source, source + n // 2):
+            blocks = [recv_ref[slots[first + i], :DATA_ROWS, :] for i in range(GROUP)]
+            halves.append(jnp.concatenate(blocks, axis=0))
+        product = dot_nt(jnp.concatenate(halves, axis=1), weights)
         for c in range(GROUP * 8):
             hit = slot_row == float(source * 8 + c)
             total = jnp.where(hit, product[8 * c : 8 * c + 8], total)

time: 32.6 us -> 32.5 us (level)
    all_to_all x1, blocking collectives: 17.3 us -> 16.8 us  [shards(): lax.all_to_all(outgoing, 'tile', split_axis=0, concat_axis=0, tiled=True,...]
    all_to_all x1, blocking collectives: 10.8 us -> 11.3 us  [shards(): lax.all_to_all(message, ('tile', 'tm'), split_axis=0, concat_axis=0, tile...]
where the time goes in v7:
time: 32.5 us; the launch traced here: 32.3 us
  blocking collectives  28.1 us (86%)
  Pallas kernels  3.52 us (11%)
  between operations  0.66 us (2%)
    all_to_all x1, blocking collectives, shards(): lax.all_to_all(outgoing, 'tile', split_axis=0, concat_axis=0, tiled=True,...  16.8 us
    all_to_all x1, blocking collectives, shards(): lax.all_to_all(message, ('tile', 'tm'), split_axis=0, concat_axis=0, tile...  11.3 us
    pallas_call x1, Pallas kernels, shards(): call(functools.partial(sweep_kernel, n, tm, slots_of(devices)), [shape((8...  1.34 us
    pallas_call x1, Pallas kernels, shards(): call(functools.partial(pack_kernel, n, slots_of(tiles)), [shape((n, DATA_...  1.29 us
    pallas_call x1, Pallas kernels, shards(): call(functools.partial(project_kernel, n, tm, slots_of(tiles), slots_of(d...  0.88 us

profile of v7, /device:TPU:0, one launch (start us, length us, event | category | flops | bytes accessed | tf_op | source)
XLA Modules:
  0.0 32.3 jit_solution(8342058039065974039)
XLA Ops:
  0.6 1.3 %shard_map.95 = (bf16[16,88,128]{2,1,0:T(8,128)(2,1)S(1)}, f32[40,128]{1,0:T(8,128)S(1)}) custom-call(s32[1,128]{1,0:T(1,128)} %bitcast.14, s32[8,128]{1,0:T(8,128)} %bitcast.10, f32[8,128]{1,0:T(8,128)} %bitcast.11, f32[8,128]{1,0:T(8,128)} %refs_3_.1, s32[8,128]{1,0:T(8,128)} %bitcast.12, s32[8,16]{1,0:T(8,128)} %bitcast.13, bf16[128,8,128]{2,1,0:T(8,128)(2,1)} %refs_6_.1), custom_call_target="tpu_custom_call" | custom-call | tf_op jit(solution)/shard_map/pallas_call | solution.py:374
  1.9 0.0 copy-start
  1.9 16.8 %all_to_all.10.recv_ref = bf16[16,88,128]{2,1,0:T(8,128)(2,1)S(1)} all-to-all(bf16[16,88,128]{2,1,0:T(8,128)(2,1)S(1)} %get-tuple-element.10), channel_id=1, replica_groups={{10,2,8,20,18,30,28,24,6,4,22,16,12,14,26,0},{11,3,9,21,19,31,29,25,7,5..., dimensions={0} | all-to-all | bytes 720896 | tf_op jit(solution)/shard_map/all_to_all | solution.py:383
  18.7 0.0 copy-done
  18.7 0.9 %shard_map.96 = (f32[32,8,128]{2,1,0:T(8,128)S(1)}, f32[8,128]{1,0:T(8,128)S(1)}, s32[32,128]{1,0:T(8,128)S(1)}, f32[96,128]{1,0:T(8,128)S(1)}) custom-call(bf16[16,88,128]{2,1,0:T(8,128)(2,1)S(1)} %all_to_all.10.recv_ref, bf16[1024,128]{1,0:T(8,128)(2,1)S(1)} %bitcast.9, f32[40,128]{1,0:T(8,128)S(1)} %get-tuple-element.11.own_ref), custom_call_target="tpu_custom_call" | custom-call | tf_op jit(solution)/shard_map/pallas_call | solution.py:387
  19.6 11.3 %all_to_all.11.recv_ref = f32[32,8,128]{2,1,0:T(8,128)S(1)} all-to-all(f32[32,8,128]{2,1,0:T(8,128)S(1)} %get-tuple-element.12), channel_id=1, replica_groups={{0,17,26,21,1,25,7,24,29,9,16,5,22,12,18,8,13,20,28,14,19,3,2,4,23,31,2..., dimensions={0} | all-to-all | bytes 262144 | tf_op jit(solution)/shard_map/all_to_all | solution.py:394
  30.9 1.3 %shard_map.97 = (f32[8,128]{1,0:T(8,128)}, f32[1,128]{1,0:T(1,128)}) custom-call(f32[32,8,128]{2,1,0:T(8,128)S(1)} %all_to_all.11.recv_ref, f32[8,128]{1,0:T(8,128)S(1)} %get-tuple-element.13.gram_ref, f32[40,128]{1,0:T(8,128)S(1)} %get-tuple-element.11.own_ref, s32[32,128]{1,0:T(8,128)S(1)} %get-tuple-element.14.lanes_ref, ...), custom_call_target="tpu_custom_call" | custom-call | tf_op jit(solution)/shard_map/pallas_call | solution.py:397
Async XLA Ops:
  1.9 16.8 %copy-start = (bf16[128,8,128]{2,1,0:T(8,128)(2,1)S(1)}, bf16[128,8,128]{2,1,0:T(8,128)(2,1)}, u32[]{:S(2)}) copy-start(bf16[128,8,128]{2,1,0:T(8,128)(2,1)} %param.11) | copy-start | bytes 786436

commit v8 on v7

--- a/solution.py
+++ b/solution.py
@@ -15,7 +15,7 @@
 NEAR = REACH[:4]
 ORDERS = {
     (16, 2): (
-        [5, 1, 4, 10, 9, 15, 14, 12, 3, 2, 11, 8, 6, 7, 13, 0],
+        [6, 4, 5, 0, 9, 15, 13, 3, 10, 2, 1, 12, 7, 14, 11, 8],
         [0, 17, 26, 21, 1, 25, 7, 24, 29, 9, 16, 5, 22, 12, 18, 8]
         + [13, 20, 28, 14, 19, 3, 2, 4, 23, 31, 27, 10, 6, 11, 15, 30],
     ),
@@ -93,11 +93,12 @@
     me = lax.axis_index("tile")
     lane = iota((8, LANES), 1)
     row = iota((8, LANES), 0)
-    for copy in copies[:5]:
+    copies[0].wait()
+    pos = places(colour_ref[...])
+    order = (iota((LANES, LANES), 0).astype(jnp.float32) == pos).astype(jnp.bfloat16)
+    for copy in copies[1:5]:
         copy.wait()
     own_ref[24:32, :] = slot_ref[...].astype(jnp.float32)
-    pos = places(colour_ref[...])
-    order = (iota((LANES, LANES), 0).astype(jnp.float32) == pos).astype(jnp.bfloat16)
     ids = corr_ref[...]
     away = jnp.bitwise_and(lax.shift_right_logical(ids, 7) - me, n - 1)
     which = jnp.where(away == 0, 0, jnp.where(away == 1, 1, jnp.where(away == n - 1, 2, 3)))

time: 32.5 us -> 32 us (0.985)
  blocking collectives: 28.1 us -> 27.7 us
    all_to_all x1, blocking collectives: 11.3 us -> 10.1 us  [shards(): lax.all_to_all(message, ('tile', 'tm'), split_axis=0, concat_axis=0, tile...]
    all_to_all x1, blocking collectives: 16.8 us -> 17.6 us  [shards(): lax.all_to_all(outgoing, 'tile', split_axis=0, concat_axis=0, tiled=True,...]
where the time goes in v8:
time: 32 us; the launch traced here: 31.8 us
  blocking collectives  27.7 us (87%)
  Pallas kernels  3.43 us (11%)
  between operations  0.66 us (2%)
    all_to_all x1, blocking collectives, shards(): lax.all_to_all(outgoing, 'tile', split_axis=0, concat_axis=0, tiled=True,...  17.6 us
    all_to_all x1, blocking collectives, shards(): lax.all_to_all(message, ('tile', 'tm'), split_axis=0, concat_axis=0, tile...  10.1 us
    pallas_call x1, Pallas kernels, shards(): call(functools.partial(sweep_kernel, n, tm, slots_of(devices)), [shape((8...  1.34 us
    pallas_call x1, Pallas kernels, shards(): call(functools.partial(pack_kernel, n, slots_of(tiles)), [shape((n, DATA_...  1.21 us
    pallas_call x1, Pallas kernels, shards(): call(functools.partial(project_kernel, n, tm, slots_of(tiles), slots_of(d...  0.88 us

profile of v8, /device:TPU:0, one launch (start us, length us, event | category | flops | bytes accessed | tf_op | source)
XLA Modules:
  0.0 31.8 jit_solution(13209215991496661343)
XLA Ops:
  0.6 1.2 %shard_map.95 = (bf16[16,88,128]{2,1,0:T(8,128)(2,1)S(1)}, f32[40,128]{1,0:T(8,128)S(1)}) custom-call(s32[1,128]{1,0:T(1,128)} %bitcast.14, s32[8,128]{1,0:T(8,128)} %bitcast.10, f32[8,128]{1,0:T(8,128)} %bitcast.11, f32[8,128]{1,0:T(8,128)} %refs_3_.1, s32[8,128]{1,0:T(8,128)} %bitcast.12, s32[8,16]{1,0:T(8,128)} %bitcast.13, bf16[128,8,128]{2,1,0:T(8,128)(2,1)} %refs_6_.1), custom_call_target="tpu_custom_call" | custom-call | tf_op jit(solution)/shard_map/pallas_call | solution.py:375
  1.8 0.0 copy-start
  1.9 17.6 %all_to_all.10.recv_ref = bf16[16,88,128]{2,1,0:T(8,128)(2,1)S(1)} all-to-all(bf16[16,88,128]{2,1,0:T(8,128)(2,1)S(1)} %get-tuple-element.10), channel_id=1, replica_groups={{12,8,10,0,18,30,26,6,20,4,2,24,14,28,22,16},{13,9,11,1,19,31,27,7,21,5..., dimensions={0} | all-to-all | bytes 720896 | tf_op jit(solution)/shard_map/all_to_all | solution.py:384
  19.5 0.0 copy-done
  19.5 0.9 %shard_map.96 = (f32[32,8,128]{2,1,0:T(8,128)S(1)}, f32[8,128]{1,0:T(8,128)S(1)}, s32[32,128]{1,0:T(8,128)S(1)}, f32[96,128]{1,0:T(8,128)S(1)}) custom-call(bf16[16,88,128]{2,1,0:T(8,128)(2,1)S(1)} %all_to_all.10.recv_ref, bf16[1024,128]{1,0:T(8,128)(2,1)S(1)} %bitcast.9, f32[40,128]{1,0:T(8,128)S(1)} %get-tuple-element.11.own_ref), custom_call_target="tpu_custom_call" | custom-call | tf_op jit(solution)/shard_map/pallas_call | solution.py:388
  20.4 10.1 %all_to_all.11.recv_ref = f32[32,8,128]{2,1,0:T(8,128)S(1)} all-to-all(f32[32,8,128]{2,1,0:T(8,128)S(1)} %get-tuple-element.12), channel_id=1, replica_groups={{0,17,26,21,1,25,7,24,29,9,16,5,22,12,18,8,13,20,28,14,19,3,2,4,23,31,2..., dimensions={0} | all-to-all | bytes 262144 | tf_op jit(solution)/shard_map/all_to_all | solution.py:395
  30.4 1.3 %shard_map.97 = (f32[8,128]{1,0:T(8,128)}, f32[1,128]{1,0:T(1,128)}) custom-call(f32[32,8,128]{2,1,0:T(8,128)S(1)} %all_to_all.11.recv_ref, f32[8,128]{1,0:T(8,128)S(1)} %get-tuple-element.13.gram_ref, f32[40,128]{1,0:T(8,128)S(1)} %get-tuple-element.11.own_ref, s32[32,128]{1,0:T(8,128)S(1)} %get-tuple-element.14.lanes_ref, ...), custom_call_target="tpu_custom_call" | custom-call | tf_op jit(solution)/shard_map/pallas_call | solution.py:398
Async XLA Ops:
  1.8 17.7 %copy-start = (bf16[128,8,128]{2,1,0:T(8,128)(2,1)S(1)}, bf16[128,8,128]{2,1,0:T(8,128)(2,1)}, u32[]{:S(2)}) copy-start(bf16[128,8,128]{2,1,0:T(8,128)(2,1)} %param.11) | copy-start | bytes 786436

commit v9 on v8

--- a/solution.py
+++ b/solution.py
@@ -15,7 +15,7 @@
 NEAR = REACH[:4]
 ORDERS = {
     (16, 2): (
-        [6, 4, 5, 0, 9, 15, 13, 3, 10, 2, 1, 12, 7, 14, 11, 8],
+        [11, 1, 14, 3, 12, 0, 10, 15, 7, 5, 13, 2, 6, 4, 8, 9],
         [0, 17, 26, 21, 1, 25, 7, 24, 29, 9, 16, 5, 22, 12, 18, 8]
         + [13, 20, 28, 14, 19, 3, 2, 4, 23, 31, 27, 10, 6, 11, 15, 30],
     ),

time: 32 us -> 31.4 us (0.981)
  blocking collectives: 27.7 us -> 27.1 us
    all_to_all x1, blocking collectives: 17.6 us -> 16.4 us  [shards(): lax.all_to_all(outgoing, 'tile', split_axis=0, concat_axis=0, tiled=True,...]
    all_to_all x1, blocking collectives: 10.1 us -> 10.7 us  [shards(): lax.all_to_all(message, ('tile', 'tm'), split_axis=0, concat_axis=0, tile...]
where the time goes in v9:
time: 31.4 us; the launch traced here: 31.2 us
  blocking collectives  27.1 us (86%)
  Pallas kernels  3.43 us (11%)
  between operations  0.66 us (2%)
    all_to_all x1, blocking collectives, shards(): lax.all_to_all(outgoing, 'tile', split_axis=0, concat_axis=0, tiled=True,...  16.4 us
    all_to_all x1, blocking collectives, shards(): lax.all_to_all(message, ('tile', 'tm'), split_axis=0, concat_axis=0, tile...  10.7 us
    pallas_call x1, Pallas kernels, shards(): call(functools.partial(sweep_kernel, n, tm, slots_of(devices)), [shape((8...  1.34 us
    pallas_call x1, Pallas kernels, shards(): call(functools.partial(pack_kernel, n, slots_of(tiles)), [shape((n, DATA_...  1.21 us
    pallas_call x1, Pallas kernels, shards(): call(functools.partial(project_kernel, n, tm, slots_of(tiles), slots_of(d...  0.88 us

profile of v9, /device:TPU:0, one launch (start us, length us, event | category | flops | bytes accessed | tf_op | source)
XLA Modules:
  0.0 31.2 jit_solution(6848653318301698763)
XLA Ops:
  0.6 1.2 %shard_map.95 = (bf16[16,88,128]{2,1,0:T(8,128)(2,1)S(1)}, f32[40,128]{1,0:T(8,128)S(1)}) custom-call(s32[1,128]{1,0:T(1,128)} %bitcast.14, s32[8,128]{1,0:T(8,128)} %bitcast.10, f32[8,128]{1,0:T(8,128)} %bitcast.11, f32[8,128]{1,0:T(8,128)} %refs_3_.1, s32[8,128]{1,0:T(8,128)} %bitcast.12, s32[8,16]{1,0:T(8,128)} %bitcast.13, bf16[128,8,128]{2,1,0:T(8,128)(2,1)} %refs_6_.1), custom_call_target="tpu_custom_call" | custom-call | tf_op jit(solution)/shard_map/pallas_call | solution.py:375
  1.8 0.0 copy-start
  1.9 16.4 %all_to_all.10.recv_ref = bf16[16,88,128]{2,1,0:T(8,128)(2,1)S(1)} all-to-all(bf16[16,88,128]{2,1,0:T(8,128)(2,1)S(1)} %get-tuple-element.10), channel_id=1, replica_groups={{22,2,28,6,24,0,20,30,14,10,26,4,12,8,16,18},{23,3,29,7,25,1,21,31,15,1..., dimensions={0} | all-to-all | bytes 720896 | tf_op jit(solution)/shard_map/all_to_all | solution.py:384
  18.3 0.0 copy-done
  18.3 0.9 %shard_map.96 = (f32[32,8,128]{2,1,0:T(8,128)S(1)}, f32[8,128]{1,0:T(8,128)S(1)}, s32[32,128]{1,0:T(8,128)S(1)}, f32[96,128]{1,0:T(8,128)S(1)}) custom-call(bf16[16,88,128]{2,1,0:T(8,128)(2,1)S(1)} %all_to_all.10.recv_ref, bf16[1024,128]{1,0:T(8,128)(2,1)S(1)} %bitcast.9, f32[40,128]{1,0:T(8,128)S(1)} %get-tuple-element.11.own_ref), custom_call_target="tpu_custom_call" | custom-call | tf_op jit(solution)/shard_map/pallas_call | solution.py:388
  19.2 10.7 %all_to_all.11.recv_ref = f32[32,8,128]{2,1,0:T(8,128)S(1)} all-to-all(f32[32,8,128]{2,1,0:T(8,128)S(1)} %get-tuple-element.12), channel_id=1, replica_groups={{0,17,26,21,1,25,7,24,29,9,16,5,22,12,18,8,13,20,28,14,19,3,2,4,23,31,2..., dimensions={0} | all-to-all | bytes 262144 | tf_op jit(solution)/shard_map/all_to_all | solution.py:395
  29.9 1.3 %shard_map.97 = (f32[8,128]{1,0:T(8,128)}, f32[1,128]{1,0:T(1,128)}) custom-call(f32[32,8,128]{2,1,0:T(8,128)S(1)} %all_to_all.11.recv_ref, f32[8,128]{1,0:T(8,128)S(1)} %get-tuple-element.13.gram_ref, f32[40,128]{1,0:T(8,128)S(1)} %get-tuple-element.11.own_ref, s32[32,128]{1,0:T(8,128)S(1)} %get-tuple-element.14.lanes_ref, ...), custom_call_target="tpu_custom_call" | custom-call | tf_op jit(solution)/shard_map/pallas_call | solution.py:398
Async XLA Ops:
  1.8 16.4 %copy-start = (bf16[128,8,128]{2,1,0:T(8,128)(2,1)S(1)}, bf16[128,8,128]{2,1,0:T(8,128)(2,1)}, u32[]{:S(2)}) copy-start(bf16[128,8,128]{2,1,0:T(8,128)(2,1)} %param.11) | copy-start | bytes 786436

commit v10 on v9

--- a/solution.py
+++ b/solution.py
@@ -25,7 +25,7 @@
 DATA_ROWS = 64
 META_ROWS = 24
 LOW_SENT = 6
-GROUP = 4
+GROUP = 8
 VMEM_LIMIT = 48 * 2 ** 20
 PACK_LIMIT = 48 * 2 ** 20
 NT = (((1,), (1,)), ((), ()))

time: 31.4 us -> 31.4 us (level)
  no operation moved by 1% of the time
where the time goes in v10:
time: 31.4 us; the launch traced here: 31.2 us
  blocking collectives  27.1 us (86%)
  Pallas kernels  3.43 us (11%)
  between operations  0.66 us (2%)
    all_to_all x1, blocking collectives, shards(): lax.all_to_all(outgoing, 'tile', split_axis=0, concat_axis=0, tiled=True,...  16.4 us
    all_to_all x1, blocking collectives, shards(): lax.all_to_all(message, ('tile', 'tm'), split_axis=0, concat_axis=0, tile...  10.7 us
    pallas_call x1, Pallas kernels, shards(): call(functools.partial(sweep_kernel, n, tm, slots_of(devices)), [shape((8...  1.34 us
    pallas_call x1, Pallas kernels, shards(): call(functools.partial(pack_kernel, n, slots_of(tiles)), [shape((n, DATA_...  1.21 us
    pallas_call x1, Pallas kernels, shards(): call(functools.partial(project_kernel, n, tm, slots_of(tiles), slots_of(d...  0.88 us

profile of v10, /device:TPU:0, one launch (start us, length us, event | category | flops | bytes accessed | tf_op | source)
XLA Modules:
  0.0 31.2 jit_solution(10614185442185478900)
XLA Ops:
  0.6 1.2 %shard_map.95 = (bf16[16,88,128]{2,1,0:T(8,128)(2,1)S(1)}, f32[40,128]{1,0:T(8,128)S(1)}) custom-call(s32[1,128]{1,0:T(1,128)} %bitcast.14, s32[8,128]{1,0:T(8,128)} %bitcast.10, f32[8,128]{1,0:T(8,128)} %bitcast.11, f32[8,128]{1,0:T(8,128)} %refs_3_.1, s32[8,128]{1,0:T(8,128)} %bitcast.12, s32[8,16]{1,0:T(8,128)} %bitcast.13, bf16[128,8,128]{2,1,0:T(8,128)(2,1)} %refs_6_.1), custom_call_target="tpu_custom_call" | custom-call | tf_op jit(solution)/shard_map/pallas_call | solution.py:375
  1.8 0.0 copy-start
  1.9 16.4 %all_to_all.10.recv_ref = bf16[16,88,128]{2,1,0:T(8,128)(2,1)S(1)} all-to-all(bf16[16,88,128]{2,1,0:T(8,128)(2,1)S(1)} %get-tuple-element.10), channel_id=1, replica_groups={{22,2,28,6,24,0,20,30,14,10,26,4,12,8,16,18},{23,3,29,7,25,1,21,31,15,1..., dimensions={0} | all-to-all | bytes 720896 | tf_op jit(solution)/shard_map/all_to_all | solution.py:384
  18.3 0.0 copy-done
  18.3 0.9 %shard_map.96 = (f32[32,8,128]{2,1,0:T(8,128)S(1)}, f32[8,128]{1,0:T(8,128)S(1)}, s32[32,128]{1,0:T(8,128)S(1)}, f32[96,128]{1,0:T(8,128)S(1)}) custom-call(bf16[16,88,128]{2,1,0:T(8,128)(2,1)S(1)} %all_to_all.10.recv_ref, bf16[1024,128]{1,0:T(8,128)(2,1)S(1)} %bitcast.9, f32[40,128]{1,0:T(8,128)S(1)} %get-tuple-element.11.own_ref), custom_call_target="tpu_custom_call" | custom-call | tf_op jit(solution)/shard_map/pallas_call | solution.py:388
  19.2 10.7 %all_to_all.11.recv_ref = f32[32,8,128]{2,1,0:T(8,128)S(1)} all-to-all(f32[32,8,128]{2,1,0:T(8,128)S(1)} %get-tuple-element.12), channel_id=1, replica_groups={{0,17,26,21,1,25,7,24,29,9,16,5,22,12,18,8,13,20,28,14,19,3,2,4,23,31,2..., dimensions={0} | all-to-all | bytes 262144 | tf_op jit(solution)/shard_map/all_to_all | solution.py:395
  29.9 1.3 %shard_map.97 = (f32[8,128]{1,0:T(8,128)}, f32[1,128]{1,0:T(1,128)}) custom-call(f32[32,8,128]{2,1,0:T(8,128)S(1)} %all_to_all.11.recv_ref, f32[8,128]{1,0:T(8,128)S(1)} %get-tuple-element.13.gram_ref, f32[40,128]{1,0:T(8,128)S(1)} %get-tuple-element.11.own_ref, s32[32,128]{1,0:T(8,128)S(1)} %get-tuple-element.14.lanes_ref, ...), custom_call_target="tpu_custom_call" | custom-call | tf_op jit(solution)/shard_map/pallas_call | solution.py:398
Async XLA Ops:
  1.8 16.4 %copy-start = (bf16[128,8,128]{2,1,0:T(8,128)(2,1)S(1)}, bf16[128,8,128]{2,1,0:T(8,128)(2,1)}, u32[]{:S(2)}) copy-start(bf16[128,8,128]{2,1,0:T(8,128)(2,1)} %param.11) | copy-start | bytes 786436
